TPU v7x, 256 devices: a whole 4x4x8 slice. The times are simulated.
256 devices in a mesh: blk: 32 (over z, y_hi, core), member: 8 (over x, y_lo).
Axes of the slice: x: 4, y: 4 (y_hi: 2, y_lo: 2; y = y_hi * 2 + y_lo), z: 8, core: 2. Of those that a mesh axis runs over, the one named last changes fastest.
Arguments:
- frames: float32 [32, 4096, 1024], P('blk', 'member'), may hold values from -6 to 6
- targets: float32 [32, 4096, 1024], P('blk', 'member'), may hold values from -6 to 6
- w_first: float32 [32, 1024, 1024], P('blk', 'member'), may hold values from -6 to 6
- w_second: float32 [32, 1024, 1024], P('blk', 'member'), may hold values from -6 to 6
Outputs:
- new_first: float32 [32, 1024, 1024], P('blk', 'member')
- new_second: float32 [32, 1024, 1024], P('blk', 'member')
All inputs are finite; a program needn't handle non-finite values.
Results may differ from a plain program's by a relative error of at most 0.000078.
Values sent between devices are 32-bit elements; how exact they have to be, the bound alone decides.
No kernel may reach another device: no remote copies, remote signals or barrier semaphores. Data moves between devices by JAX's collectives and lax.ppermute only.
A program may use at most 128 MiB of HBM per device.

v0:
```python
import jax
import jax.numpy as jnp
from jax import lax
from jax.sharding import Mesh
from jax.sharding import PartitionSpec as P

MEMBER = ("member_0", "member_1")


learn_rate = 300.0


def passed_along(x, axis, by):
    devices = lax.axis_size(axis)
    return lax.ppermute(x, axis, [(i, (i + by) % devices) for i in range(devices)])


def whole_of(x, axes, dim):
    filled = x
    for number in range(len(axes) - 1, -1, -1):
        filled = lax.all_gather(filled, axes[number], axis=dim, tiled=True)
    return filled


def cut_along(x, dim, devices):
    lengths = x.shape
    blocks = x.reshape(*lengths[:dim], devices, lengths[dim] // devices, *lengths[dim + 1 :])
    return jnp.moveaxis(blocks, dim, 0)


def sent_and_summed(x, axis, dim):
    devices = lax.axis_size(axis)
    blocks = lax.all_to_all(cut_along(x, dim, devices), axis, 0, 0, tiled=True)
    return jnp.sum(blocks, axis=0)


def neighbours(own_first, own_second):
    below = passed_along((own_first, own_second), "blk", 1)
    above = passed_along((own_first, own_second), "blk", -1)
    return (below, above)


def body(frames, targets, w_first, w_second):
    high = lax.Precision.HIGHEST
    inputs = frames[0]
    goal = targets[0]
    own_first = w_first[0]
    own_second = w_second[0]
    members = lax.axis_size(MEMBER)
    total_frames = inputs.shape[0] * members
    width_in = inputs.shape[1]
    width_hid = own_first.shape[1]
    scale_in = width_in ** (-0.5)
    scale_hid = width_hid ** (-0.5)
    columns = inputs
    pre_first = (
        jnp.dot(
            columns,
            whole_of(own_first, MEMBER, 0),
            precision=high,
            preferred_element_type=jnp.float32,
        )
        * scale_in
    )
    sig = jax.nn.sigmoid(pre_first)
    hidden = pre_first * sig
    slope = sig * (1.0 + pre_first * (1.0 - sig))
    whole_second = whole_of(own_second, MEMBER, 0)
    output = (
        jnp.dot(hidden, whole_second, precision=high, preferred_element_type=jnp.float32)
        * scale_hid
    )
    delta_out = (output - goal) / total_frames
    columns = hidden
    grad_second = sent_and_summed(
        lax.dot_general(
            columns,
            delta_out,
            (((0,), (0,)), ((), ())),
            precision=high,
            preferred_element_type=jnp.float32,
        )
        * scale_hid,
        MEMBER,
        0,
    )
    back = (
        lax.dot_general(
            delta_out,
            whole_second,
            (((1,), (1,)), ((), ())),
            precision=high,
            preferred_element_type=jnp.float32,
        )
        * scale_hid
    )
    delta_hidden = back * slope
    columns = inputs
    grad_first = sent_and_summed(
        lax.dot_general(
            columns,
            delta_hidden,
            (((0,), (0,)), ((), ())),
            precision=high,
            preferred_element_type=jnp.float32,
        )
        * scale_in,
        MEMBER,
        0,
    )
    below, above = neighbours(own_first, own_second)
    mixed_first = (below[0] + own_first + above[0]) / 3.0
    mixed_second = (below[1] + own_second + above[1]) / 3.0
    new_first = mixed_first - learn_rate * grad_first
    new_second = mixed_second - learn_rate * grad_second
    return (new_first[None], new_second[None])


def solution(mesh):
    torus = Mesh(mesh.devices.reshape(mesh.shape["blk"], 4, 2), ("blk", "member_0", "member_1"))
    return jax.shard_map(
        body,
        mesh=torus,
        in_specs=(
            P("blk", MEMBER, None),
            P("blk", MEMBER, None),
            P("blk", MEMBER, None),
            P("blk", MEMBER, None),
        ),
        out_specs=(P("blk", MEMBER, None), P("blk", MEMBER, None)),
        check_vma=False,
    )
```

profile of v0, /device:TPU:1, one launch (start us, length us, event | category | flops | bytes accessed | tf_op | source)
XLA Modules:
  0.0 345.7 jit_solution(5288896465629789746)
XLA Ops:
  7.2 0.0 copy-start
  7.2 0.0 all-gather.9.cloned.1.call-start
  7.2 0.7 all-gather.9.cloned.1.call-update
  7.9 0.0 all-gather.13.cloned.1.call-start
  8.0 0.7 all-gather.13.cloned.1.call-update
  8.7 0.0 all-gather.11.cloned.1.call-start
  8.7 31.3 %all-gather.9.cloned.1.call-done = f32[1,256,1024]{2,1,0:T(8,128)} async-done(((f32[1,128,1024]{2,1,0:T(8,128)}), f32[1,256,1024]{2,1,0:T(8,128)}) %all-gather.9.cloned.1.call-update) | async-done | bytes 1048592 | tf_op jit(solution)/shard_map/all_gather | solution.py:21
  40.0 0.0 all-gather.11.cloned.1.call-update
  40.1 0.0 all-gather.15.cloned.1.call-start
  40.1 29.2 %all-gather.13.cloned.1.call-done = f32[1,256,1024]{2,1,0:T(8,128)} async-done(((f32[1,128,1024]{2,1,0:T(8,128)}), f32[1,256,1024]{2,1,0:T(8,128)}) %all-gather.13.cloned.1.call-update) | async-done | bytes 1048592 | tf_op jit(solution)/shard_map/all_gather | solution.py:21
  69.3 0.0 all-gather.15.cloned.1.call-update
  69.3 53.6 %all-gather.11.cloned.1.call-done = f32[1,1024,1024]{2,1,0:T(8,128)} async-done(((f32[1,256,1024]{2,1,0:T(8,128)}), f32[1,1024,1024]{2,1,0:T(8,128)}) %all-gather.11.cloned.1.call-update) | async-done | bytes 4194320 | tf_op jit(solution)/shard_map/all_gather | solution.py:21
  122.9 0.0 copy-done
  122.9 9.7 %fusion.4 = f32[512,1024]{1,0:T(8,128)} fusion(f32[1,1024,1024]{2,1,0:T(8,128)} %all-gather.11.cloned.1.call-done, f32[1,512,1024]{2,1,0:T(8,128)S(1)} %copy-done), kind=kOutput, calls=%fused_computation.5 | convolution fusion | flops 6442450944 | bytes 8388608 | tf_op jit(solution)/shard_map/dot_general | solution.py:57
  132.6 43.2 %all-gather.15.cloned.1.call-done = f32[1,1024,1024]{2,1,0:T(8,128)} async-done(((f32[1,256,1024]{2,1,0:T(8,128)}), f32[1,1024,1024]{2,1,0:T(8,128)}) %all-gather.15.cloned.1.call-update) | async-done | bytes 4194320 | tf_op jit(solution)/shard_map/all_gather | solution.py:21
  175.8 0.0 copy-start.3
  175.8 11.8 %fusion.6 = f32[512,1024]{1,0:T(8,128)S(1)} fusion(f32[1,512,1024]{2,1,0:T(8,128)} %param.5, f32[1,1024,1024]{2,1,0:T(8,128)} %all-gather.15.cloned.1.call-done, f32[512,1024]{1,0:T(8,128)} %fusion.4), kind=kOutput, calls=%fused_computation.10 | convolution fusion | flops 6446645248 | bytes 10485760 | tf_op jit(solution)/shard_map/dot_general | solution.py:70
  187.6 0.0 copy-done.3
  187.6 0.0 copy-start.5
  187.6 7.0 %multiply_bitcast_fusion = f32[128,8,8,128]{3,2,1,0:T(8,128)S(1)} fusion(f32[512,1024]{1,0:T(8,128)S(1)} %fusion.6, f32[512,1024]{1,0:T(8,128)S(1)} %copy-done.3), kind=kOutput, calls=%fused_computation.7 | convolution fusion | flops 6446120960 | bytes 8388608 | tf_op jit(solution)/shard_map/dot_general | solution.py:76
  194.6 0.0 copy-done.5
  194.7 2.2 copy.22
  196.9 4.8 %all-to-all-start.1 = ((f32[8,128,1024]{1,2,0:T(8,128)}), f32[8,128,1024]{1,2,0:T(8,128)}, u32[]{:S(2)}, u32[]{:S(2)}) async-start(f32[8,128,1024]{1,2,0:T(8,128)} %bitcast.37), calls=%async_computation.1 | async-start | bytes 8388608 | tf_op jit(solution)/shard_map/all_to_all | solution.py:33
  201.7 0.0 copy-start.4
  201.7 9.8 %fusion = f32[512,1024]{1,0:T(8,128)S(1)} fusion(f32[512,1024]{1,0:T(8,128)} %copy-done.5, f32[1,1024,1024]{2,1,0:T(8,128)} %all-gather.15.cloned.1.call-done), kind=kOutput, calls=%fused_computation.1 | convolution fusion | flops 6442450944 | bytes 8388608 | tf_op jit(solution)/shard_map/dot_general | solution.py:88
  211.5 0.0 copy-done.4
  211.6 10.3 %convolution_multiply_fusion = f32[1024,1024]{0,1:T(8,128)} fusion(f32[1,512,1024]{2,1,0:T(8,128)S(1)} %copy-done, f32[512,1024]{1,0:T(8,128)S(1)} %fusion, f32[512,1024]{1,0:T(8,128)S(1)} %copy-done.4), kind=kOutput, calls=%fused_computation.8 | convolution fusion | flops 6448742400 | bytes 10485760 | tf_op jit(solution)/shard_map/dot_general | solution.py:100
  221.8 38.9 %all-to-all-done.1 = f32[8,128,1024]{1,2,0:T(8,128)} async-done(((f32[8,128,1024]{1,2,0:T(8,128)}), f32[8,128,1024]{1,2,0:T(8,128)}, u32[]{:S(2)}, u32[]{:S(2)}) %all-to-all-start.1) | async-done | bytes 4194336 | tf_op jit(solution)/shard_map/all_to_all | solution.py:33
  260.7 0.0 copy-start.1
  260.7 4.7 %all-to-all-start = ((f32[8,128,1024]{2,1,0:T(8,128)}), f32[8,128,1024]{2,1,0:T(8,128)}, u32[]{:S(2)}, u32[]{:S(2)}) async-start(f32[8,128,1024]{2,1,0:T(8,128)} %bitcast.38), calls=%async_computation | async-start | bytes 8388608 | tf_op jit(solution)/shard_map/all_to_all | solution.py:33
  265.5 0.0 copy-done.1
  265.5 4.2 %collective-permute-start = (f32[128,1024]{1,0:T(8,128)S(1)}, f32[128,1024]{1,0:T(8,128)}, u32[]{:S(2)}, u32[]{:S(2)}) collective-permute-start(f32[128,1024]{1,0:T(8,128)S(1)} %bitcast.39), channel_id=1, source_target_pairs={{0,8},{8,16},{16,24},{24,32},{32,40},{40,48},{48,56},{56,64},{64,7... | collective-permute-start | bytes 1572872 | tf_op jit(solution)/shard_map/ppermute | solution.py:15
  269.6 0.0 collective-permute-start.1
  269.6 3.2 collective-permute-start.2
  272.9 0.0 collective-permute-start.3
  272.9 2.4 reduce_sum.19
  275.3 1.0 copy.17
  276.3 53.8 %all-to-all-done = f32[8,128,1024]{2,1,0:T(8,128)} async-done(((f32[8,128,1024]{2,1,0:T(8,128)}), f32[8,128,1024]{2,1,0:T(8,128)}, u32[]{:S(2)}, u32[]{:S(2)}) %all-to-all-start) | async-done | bytes 4194336 | tf_op jit(solution)/shard_map/all_to_all | solution.py:33
  330.1 2.6 reduce_sum.18
  332.8 0.0 copy-start.2
  332.8 0.0 collective-permute-done
  332.8 0.0 collective-permute-done.1
  332.8 2.2 subtract_bitcast_fusion.1
  335.0 0.0 collective-permute-done.2
  335.0 1.8 collective-permute-done.3
  336.8 0.0 copy-done.2
  336.8 2.3 subtract_bitcast_fusion
Async XLA Ops:
  7.2 115.7 %copy-start = (f32[1,512,1024]{2,1,0:T(8,128)S(1)}, f32[1,512,1024]{2,1,0:T(8,128)}, u32[]{:S(2)}) copy-start(f32[1,512,1024]{2,1,0:T(8,128)} %param.4) | copy-start | bytes 6291460
  7.2 32.9 %all-gather.9.cloned.1.call-start = ((), (), s32[]{:S(2)}) async-start(), calls=%async_computation.2 | async-start | bytes 1572864 | tf_op jit(solution)/shard_map/all_gather | solution.py:21
  7.9 61.4 %all-gather.13.cloned.1.call-start = ((), (), s32[]{:S(2)}) async-start(), calls=%async_computation.4 | async-start | bytes 1572864 | tf_op jit(solution)/shard_map/all_gather | solution.py:21
  8.7 114.2 %all-gather.11.cloned.1.call-start = ((), (), s32[]{:S(2)}) async-start(), calls=%async_computation.3 | async-start | bytes 5242880 | tf_op jit(solution)/shard_map/all_gather | solution.py:21
  40.1 135.7 %all-gather.15.cloned.1.call-start = ((), (), s32[]{:S(2)}) async-start(), calls=%async_computation.5 | async-start | bytes 5242880 | tf_op jit(solution)/shard_map/all_gather | solution.py:21
  175.8 11.8 %copy-start.3 = (f32[512,1024]{1,0:T(8,128)S(1)}, f32[512,1024]{1,0:T(8,128)}, u32[]{:S(2)}) copy-start(f32[512,1024]{1,0:T(8,128)} %fusion.4) | copy-start | bytes 6291460
  187.6 7.0 %copy-start.5 = (f32[512,1024]{1,0:T(8,128)}, f32[512,1024]{1,0:T(8,128)S(1)}, u32[]{:S(2)}) copy-start(f32[512,1024]{1,0:T(8,128)S(1)} %fusion.6) | copy-start | bytes 6291460
  196.9 63.8 %all-to-all-start.1 = ((f32[8,128,1024]{1,2,0:T(8,128)}), f32[8,128,1024]{1,2,0:T(8,128)}, u32[]{:S(2)}, u32[]{:S(2)}) async-start(f32[8,128,1024]{1,2,0:T(8,128)} %bitcast.37), calls=%async_computation.1 | async-start | bytes 8388608 | tf_op jit(solution)/shard_map/all_to_all | solution.py:33
  201.7 9.9 %copy-start.4 = (f32[512,1024]{1,0:T(8,128)S(1)}, f32[512,1024]{1,0:T(8,128)}, u32[]{:S(2)}) copy-start(f32[512,1024]{1,0:T(8,128)} %fusion.4) | copy-start | bytes 6291460
  260.7 4.8 %copy-start.1 = (f32[1,128,1024]{2,1,0:T(8,128)S(1)}, f32[1,128,1024]{2,1,0:T(8,128)}, u32[]{:S(2)}) copy-start(f32[1,128,1024]{2,1,0:T(8,128)} %param.6) | copy-start | bytes 1572868
  260.7 69.4 %all-to-all-start = ((f32[8,128,1024]{2,1,0:T(8,128)}), f32[8,128,1024]{2,1,0:T(8,128)}, u32[]{:S(2)}, u32[]{:S(2)}) async-start(f32[8,128,1024]{2,1,0:T(8,128)} %bitcast.38), calls=%async_computation | async-start | bytes 8388608 | tf_op jit(solution)/shard_map/all_to_all | solution.py:33
  265.5 67.3 %collective-permute-start = (f32[128,1024]{1,0:T(8,128)S(1)}, f32[128,1024]{1,0:T(8,128)}, u32[]{:S(2)}, u32[]{:S(2)}) collective-permute-start(f32[128,1024]{1,0:T(8,128)S(1)} %bitcast.39), channel_id=1, source_target_pairs={{0,8},{8,16},{16,24},{24,32},{32,40},{40,48},{48,56},{56,64},{64,7... | collective-permute-start | bytes 1572872 | tf_op jit(solution)/shard_map/ppermute | solution.py:15
  269.6 63.2 %collective-permute-start.1 = (f32[128,1024]{1,0:T(8,128)S(1)}, f32[128,1024]{1,0:T(8,128)}, u32[]{:S(2)}, u32[]{:S(2)}) collective-permute-start(f32[128,1024]{1,0:T(8,128)S(1)} %bitcast.40), channel_id=1, source_target_pairs={{0,248},{8,0},{16,8},{24,16},{32,24},{40,32},{48,40},{56,48},{64,5... | collective-permute-start | bytes 1572872 | tf_op jit(solution)/shard_map/ppermute | solution.py:15
  269.6 65.4 %collective-permute-start.2 = (f32[128,1024]{1,0:T(8,128)}, f32[128,1024]{1,0:T(8,128)}, u32[]{:S(2)}, u32[]{:S(2)}) collective-permute-start(f32[128,1024]{1,0:T(8,128)} %bitcast.8), channel_id=1, source_target_pairs={{0,8},{8,16},{16,24},{24,32},{32,40},{40,48},{48,56},{56,64},{64,7... | collective-permute-start | bytes 1572872 | tf_op jit(solution)/shard_map/ppermute | solution.py:15
  272.9 64.0 %collective-permute-start.3 = (f32[128,1024]{1,0:T(8,128)}, f32[128,1024]{1,0:T(8,128)}, u32[]{:S(2)}, u32[]{:S(2)}) collective-permute-start(f32[128,1024]{1,0:T(8,128)} %bitcast.8), channel_id=1, source_target_pairs={{0,248},{8,0},{16,8},{24,16},{32,24},{40,32},{48,40},{56,48},{64,5... | collective-permute-start | bytes 1572872 | tf_op jit(solution)/shard_map/ppermute | solution.py:15
  332.8 4.1 %copy-start.2 = (f32[128,1024]{1,0:T(8,128)S(1)}, f32[128,1024]{1,0:T(8,128)}, u32[]{:S(2)}) copy-start(f32[128,1024]{1,0:T(8,128)} %copy.17) | copy-start | bytes 1572868
Sparse Core Ops, SparseCore 0:
  9.8 30.1 all-gather.8
  41.8 27.3 all-gather.12
  71.1 51.7 all-gather.10
  124.6 51.1 all-gather.14
where the time goes:
time: 350 us; the launch traced here: 346 us
  waiting for transfers between devices  253 us (72%)
  matrix products  48.6 us (14%)
  starting transfers between devices  17.1 us (5%)
  between operations  13.9 us (4%)
  other arithmetic  9.58 us (3%)
    all_gather x4, waiting for transfers between devices, whole_of(): filled = lax.all_gather(filled, axes[number], axis=dim, tiled=True)  157 us
    all_to_all x2, waiting for transfers between devices, sent_and_summed(): blocks = lax.all_to_all(cut_along(x, dim, devices), axis, 0, 0, tiled=True)  92.7 us
    dot_general x1, matrix products, body(): jnp.dot(hidden, whole_second, precision=high, preferred_element_type=jnp....  11.8 us
    dot_general x1, matrix products, body(): lax.dot_general(columns, delta_hidden, (((0,), (0,)), ((), ())), precisio...  10.3 us
    dot_general x1, matrix products, body(): lax.dot_general(delta_out, whole_second, (((1,), (1,)), ((), ())), precis...  9.85 us
    dot_general x1, matrix products, body(): jnp.dot(columns, whole_of(own_first, MEMBER, 0), precision=high, preferre...  9.67 us
    all_to_all x2, starting transfers between devices, sent_and_summed(): blocks = lax.all_to_all(cut_along(x, dim, devices), axis, 0, 0, tiled=True)  9.51 us
    ppermute x4, starting transfers between devices, passed_along(): lax.ppermute(x, axis, [(i, (i + by) % devices) for i in range(devices)])  7.41 us
  transfers between devices with their start and end apart: 10, of which 7 were waited for; matrix products, arithmetic and copies ran while one was open for 11% of the time, Pallas kernels for 0%

commit v1 on v0

v1 whole, which is shorter than its diff:
```python
import functools

import jax
import jax.numpy as jnp
from jax import lax
from jax.experimental import pallas as pl
from jax.experimental.pallas import tpu as pltpu
from jax.sharding import Mesh
from jax.sharding import PartitionSpec as P

RATE = 300.0
F32 = jnp.float32
BF16 = jnp.bfloat16
TILE = 256

VMEM = pl.BlockSpec(memory_space=pltpu.VMEM)
SMEM = pl.BlockSpec(memory_space=pltpu.SMEM)
HBM = pl.BlockSpec(memory_space=pltpu.HBM)


def split(a):
    high = a.astype(BF16)
    return high, (a - high.astype(F32)).astype(BF16)


def dot(a, b, dims=((1,), (0,))):
    return lax.dot_general(a, b, (dims, ((), ())), preferred_element_type=F32)


def dot3(ah, al, bh, bl, dims=((1,), (0,))):
    return dot(ah, bl, dims) + dot(al, bh, dims) + dot(ah, bh, dims)


def params(flops, moved):
    return dict(
        compiler_params=pltpu.CompilerParams(vmem_limit_bytes=30 * 2**20),
        cost_estimate=pl.CostEstimate(flops=flops, bytes_accessed=moved, transcendentals=0),
    )


class Taken:
    def __init__(self, at_ref, own, sent, into, sem):
        self.wait = pltpu.make_async_copy(own, into, sem).wait

        @pl.when(at_ref[2] == 1)
        def _():
            pltpu.make_async_copy(sent, into, sem).start()

        @pl.when(at_ref[2] == 0)
        def _():
            pltpu.make_async_copy(own, into, sem).start()


def place(at_ref, gathered, high_ref, low_ref):
    x, core = at_ref[0], at_ref[1]
    way = 1 - 2 * core
    rows = gathered.shape[1]
    for number in range(8):
        step, other = number % 4, number // 4
        part = core if other == 0 else 1 - core
        chip = lax.rem(x - way * step + 4 if other == 0 else x + way * step + 4, 4)
        start = pl.multiple_of((chip * 2 + part) * rows, rows)
        high, low = split(gathered[number])
        high_ref[pl.ds(start, rows), :] = high
        low_ref[pl.ds(start, rows), :] = low


def fetch_weights(mine, theirs, raw, sem):
    copies = [
        pltpu.make_async_copy(a, raw.at[pl.ds(4 * i, 4)], sem.at[i]) for i, a in enumerate((mine, theirs))
    ]
    for copy in copies:
        copy.start()
    return copies


def first_kernel(scale, at_ref, own, sent, mine, theirs, *refs):
    hid_h, hid_l, hidt_h, hidt_l, slope, xt_h, xt_l, x, xh, xl, raw, wh, wl, sem = refs
    width = x.shape[1]
    taken = Taken(at_ref, own.at[:, pl.ds(0, width)], sent.at[:, pl.ds(0, width)], x, sem.at[2])
    copies = fetch_weights(mine, theirs, raw, sem)
    taken.wait()
    high, low = split(x[...])
    xh[...] = high
    xl[...] = low
    for copy in copies:
        copy.wait()
    place(at_ref, raw, wh, wl)
    for n in range(slope.shape[1] // TILE):
        cut = slice(n * TILE, (n + 1) * TILE)
        pre = dot3(xh[...], xl[...], wh[:, cut], wl[:, cut]) * scale
        sig = 1.0 / (1.0 + jnp.exp(-pre))
        hidden = pre * sig
        slope[:, cut] = sig * (1.0 + pre * (1.0 - sig))
        high, low = split(hidden)
        hid_h[:, cut] = high
        hid_l[:, cut] = low
        hidt_h[cut, :] = high.T
        hidt_l[cut, :] = low.T
        xt_h[cut, :] = xh[:, cut].T
        xt_l[cut, :] = xl[:, cut].T


def first_layer(at, own, sent, mine, theirs, scale):
    rows, width = own.shape[0], 8 * mine.shape[1]
    hid = mine.shape[2]
    shapes = [((rows, hid), BF16)] * 2 + [((hid, rows), BF16)] * 2
    shapes += [((rows, hid), F32)] + [((width, rows), BF16)] * 2
    return pl.pallas_call(
        functools.partial(first_kernel, scale),
        in_specs=[SMEM] + [HBM] * 4,
        out_specs=[VMEM] * len(shapes),
        out_shape=[jax.ShapeDtypeStruct(*s) for s in shapes],
        scratch_shapes=[
            pltpu.VMEM((rows, width), F32),
            pltpu.VMEM((rows, width), BF16),
            pltpu.VMEM((rows, width), BF16),
            pltpu.VMEM((8,) + mine.shape[1:], F32),
            pltpu.VMEM((width, hid), BF16),
            pltpu.VMEM((width, hid), BF16),
            pltpu.SemaphoreType.DMA((3,)),
        ],
        name="first_layer",
        **params(6 * rows * width * hid, 16 * 2**20),
    )(at, own, sent, mine, theirs)


def second_kernel(scale, at_ref, hid_h, hid_l, mine, theirs, out, wh, wl, raw, sem):
    for copy in fetch_weights(mine, theirs, raw, sem):
        copy.wait()
    place(at_ref, raw, wh, wl)
    for n in range(out.shape[1] // TILE):
        cut = slice(n * TILE, (n + 1) * TILE)
        out[:, cut] = dot3(hid_h[...], hid_l[...], wh[:, cut], wl[:, cut]) * scale


def second_layer(at, hid_h, hid_l, mine, theirs, scale):
    rows, hid = hid_h.shape
    width = mine.shape[2]
    return pl.pallas_call(
        functools.partial(second_kernel, scale),
        in_specs=[SMEM, VMEM, VMEM, HBM, HBM],
        out_specs=[VMEM] * 3,
        out_shape=[
            jax.ShapeDtypeStruct((rows, width), F32),
            jax.ShapeDtypeStruct((hid, width), BF16),
            jax.ShapeDtypeStruct((hid, width), BF16),
        ],
        scratch_shapes=[pltpu.VMEM((8,) + mine.shape[1:], F32), pltpu.SemaphoreType.DMA((2,))],
        name="second_layer",
        **params(6 * rows * width * hid, 12 * 2**20),
    )(at, hid_h, hid_l, mine, theirs)


def hand_out(at_ref, total, keep, send):
    x, core = at_ref[0], at_ref[1]
    way = 1 - 2 * core
    half = keep.shape[1]
    for k in range(4):
        ahead = lax.rem(x + way * k + 4, 4) * 2
        behind = lax.rem(x - way * k + 4, 4) * 2
        keep[k] = total[pl.ds(pl.multiple_of((ahead + core) * half, half), half), :]
        send[k] = total[pl.ds(pl.multiple_of((behind + 1 - core) * half, half), half), :]


def delta_kernel(frames, scale, begun, start, at_ref, out, own, sent, hidt_h, hidt_l, wh, wl, *refs):
    back_in = refs[0] if begun else None
    keep, send, back, goal, dh, dl, total, sem = refs[1 if begun else 0 :]
    columns = goal.shape[1]
    cut = slice(start, start + columns)
    there = pl.ds(start, columns)
    Taken(at_ref, own.at[:, there], sent.at[:, there], goal, sem).wait()
    high, low = split((out[:, cut] - goal[...]) / frames)
    dh[...] = high
    dl[...] = low
    for n in range(columns // TILE):
        part = slice(n * TILE, (n + 1) * TILE)
        total[:, part] = dot3(hidt_h[...], hidt_l[...], dh[:, part], dl[:, part]) * scale
    hand_out(at_ref, total, keep, send)
    for n in range(back.shape[1] // TILE):
        part = slice(n * TILE, (n + 1) * TILE)
        more = dot3(dh[...], dl[...], wh[part, cut], wl[part, cut], ((1,), (1,)))
        back[:, part] = back_in[:, part] + more if begun else more


def delta_and_second(at, start, columns, out, own, sent, hidt_h, hidt_l, wh, wl, back_in, frames, scale):
    rows = out.shape[0]
    hid = hidt_h.shape[0]
    begun = back_in is not None
    return pl.pallas_call(
        functools.partial(delta_kernel, frames, scale, begun, start),
        in_specs=[SMEM, VMEM, HBM, HBM] + [VMEM] * (5 if begun else 4),
        out_specs=[VMEM] * 3,
        out_shape=[
            jax.ShapeDtypeStruct((4, hid // 8, columns), F32),
            jax.ShapeDtypeStruct((4, hid // 8, columns), F32),
            jax.ShapeDtypeStruct((rows, hid), F32),
        ],
        scratch_shapes=[
            pltpu.VMEM((rows, columns), F32),
            pltpu.VMEM((rows, columns), BF16),
            pltpu.VMEM((rows, columns), BF16),
            pltpu.VMEM((hid, columns), F32),
            pltpu.SemaphoreType.DMA,
        ],
        name="delta_and_second",
        **params(12 * rows * columns * hid, 12 * 2**20),
    )(at, out, own, sent, hidt_h, hidt_l, wh, wl, *([back_in] if begun else []))


def grad_first_kernel(scale_hid, scale_in, start, at_ref, back, slope, xt_h, xt_l, keep, send, total):
    for n in range(total.shape[1] // TILE):
        part = slice(n * TILE, (n + 1) * TILE)
        cut = slice(start + n * TILE, start + (n + 1) * TILE)
        high, low = split((back[:, cut] * scale_hid) * slope[:, cut])
        total[:, part] = dot3(xt_h[...], xt_l[...], high, low) * scale_in
    hand_out(at_ref, total, keep, send)


def grad_first(at, start, columns, back, slope, xt_h, xt_l, scale_hid, scale_in):
    rows, hid = back.shape
    width = xt_h.shape[0]
    return pl.pallas_call(
        functools.partial(grad_first_kernel, scale_hid, scale_in, start),
        in_specs=[SMEM] + [VMEM] * 4,
        out_specs=[VMEM] * 2,
        out_shape=[jax.ShapeDtypeStruct((4, width // 8, columns), F32)] * 2,
        scratch_shapes=[pltpu.VMEM((width, columns), F32)],
        name="grad_first",
        **params(6 * rows * columns * width, 6 * 2**20),
    )(at, back, slope, xt_h, xt_l)


def round_x(a):
    n = lax.axis_size("x")
    pairs = [(i, (i + 1) % n) for i in range(n)] + [(n + i, n + (i - 1) % n) for i in range(n)]
    return lax.ppermute(a, ("core", "x"), pairs)


def to_other_core(a):
    return lax.ppermute(a, "core", [(0, 1), (1, 0)])


def across(a):
    return lax.ppermute(a, ("core", "y_lo"), [(1, 2), (2, 1)])


def next_door(a):
    n = lax.axis_size("z") * 4
    pairs = [(i, (i + 1) % n) for i in range(1, n, 2)]
    return lax.ppermute(a, ("z", "y_hi", "y_lo"), pairs + [(j, i) for i, j in pairs])


def after(value, *others):
    return lax.optimization_barrier((value, *others))[0]


def body(frames, targets, w_first, w_second):
    inputs, goal = frames[0], targets[0]
    own_first, own_second = w_first[0], w_second[0]
    total_frames = inputs.shape[0] * 8
    width, hid = inputs.shape[1], own_first.shape[1]
    scale_in, scale_hid = width ** (-0.5), hid ** (-0.5)
    half = width // 2
    core = lax.axis_index("core")
    moves = core != lax.axis_index("y_lo")
    at = jnp.stack([lax.axis_index("x"), core, moves]).astype(jnp.int32)

    got_first, got_second = across(own_first), across(own_second)
    ring = [jnp.where(moves, got_first, own_first)]
    ring2 = [jnp.where(moves, got_second, own_second)]
    sent = across(after(inputs, got_second))
    sent_goal = across(after(goal, got_second))

    for _ in range(2):
        ring.append(round_x(ring[-1]))
        ring2.append(round_x(ring2[-1]))
    far_first = next_door(ring[0])
    ring.append(round_x(ring[2]))
    ring2.append(round_x(after(ring2[2], sent)))
    mine = jnp.stack(ring)
    mine2 = jnp.stack(ring2)
    theirs = to_other_core(mine)
    mine2, far_first, sent_goal = lax.optimization_barrier((mine2, far_first, sent_goal))
    theirs2 = to_other_core(mine2)

    hid_h, hid_l, hidt_h, hidt_l, slope, xt_h, xt_l = first_layer(at, inputs, sent, mine, theirs, scale_in)
    out, wh, wl = second_layer(at, hid_h, hid_l, mine2, theirs2, scale_hid)

    def delta(start, own, sent, back):
        keep, send, back = delta_and_second(
            at, start, half, out, own, sent, hidt_h, hidt_l, wh, wl, back, total_frames, scale_hid
        )
        return keep, to_other_core(send), back

    def first(start, back):
        keep, send = grad_first(at, start, half, back, slope, xt_h, xt_l, scale_hid, scale_in)
        return keep, to_other_core(send)

    def term(keeps, sents, k):
        return jnp.concatenate([a[k] + b[k] for a, b in zip(keeps, sents)], 1)

    keep0, sent0, back = delta(0, goal, sent_goal, None)
    keep1, sent1, back = delta(half, goal, sent_goal, back)
    far_second = next_door(after(ring2[0], back))
    second = (keep0, keep1), (sent0, sent1)
    m = term(*second, 3)
    keep2, sent2 = first(0, after(back, m))
    keep3, sent3 = first(half, back)
    firsts = (keep2, keep3), (sent2, sent3)
    p = term(*firsts, 3)
    m = round_x(m) + term(*second, 2)
    p = round_x(p) + term(*firsts, 2)
    m = round_x(m) + term(*second, 1)
    p = round_x(after(p, far_second)) + term(*firsts, 1)
    m = round_x(m) + term(*second, 0)
    update_second = far_second / 3.0 - RATE * m
    near_first, near_second = ((w + to_other_core(after(w, back))) / 3.0 for w in (own_first, own_second))
    p, update_second, near_first, near_second = lax.optimization_barrier((p, update_second, near_first, near_second))
    p = round_x(p) + term(*firsts, 0)
    update_first = far_first / 3.0 - RATE * p
    new = []
    for near, update in ((near_first, update_first), (near_second, update_second)):
        new.append((near + jnp.where(moves, across(update), update))[None])
    return tuple(new)


def solution(mesh):
    torus = Mesh(
        mesh.devices.reshape(mesh.shape["blk"] // 4, 2, 2, 4, 2), ("z", "y_hi", "core", "x", "y_lo")
    )
    spec = P(("z", "y_hi", "core"), ("x", "y_lo"), None)
    return jax.shard_map(
        body, mesh=torus, in_specs=(spec,) * 4, out_specs=(spec, spec), check_vma=False
    )
```

time: 350 us -> 158 us (0.45); the launches traced: 346 us -> 158 us
  waiting for transfers between devices: 253 us -> 63.1 us
  matrix products: 48.6 us -> 0 us
  starting transfers between devices: 17.1 us -> 53.3 us
  Pallas kernels: 0 us -> 30.1 us
  between operations: 13.9 us -> 0.92 us
    all_gather x4 -> x0, waiting for transfers between devices: 157 us -> none  [whole_of(): filled = lax.all_gather(filled, axes[number], axis=dim, tiled=True)]
    all_to_all x2 -> x0, waiting for transfers between devices: 92.7 us -> none  [sent_and_summed(): blocks = lax.all_to_all(cut_along(x, dim, devices), axis, 0, 0, tiled=True)]
    ppermute x4 -> x28, waiting for transfers between devices: 1.84 us -> 63.1 us  [the longest x12 38.7 us: round_x(): return lax.ppermute(a, ('core', 'x'), pairs)]
    dot_general x5 -> x0, matrix products: 48.6 us -> none  [the longest x1 11.8 us: body(): jnp.dot(hidden, whole_second, precision=high, preferred_element_type=jnp....]
    ppermute x4 -> x28, starting transfers between devices: 7.41 us -> 53.3 us  [the longest x12 18.9 us: round_x(): return lax.ppermute(a, ('core', 'x'), pairs)]
    pallas_call x0 -> x6, Pallas kernels: none -> 30.1 us  [the longest x2 9.02 us: delta_and_second(): pl.pallas_call(functools.partial(delta_kernel, frames, scale, begun, star...]
    all_to_all x2 -> x0, starting transfers between devices: 9.51 us -> none  [sent_and_summed(): blocks = lax.all_to_all(cut_along(x, dim, devices), axis, 0, 0, tiled=True)]
    reduce_sum x2 -> x0, other arithmetic: 5.06 us -> none  [sent_and_summed(): return jnp.sum(blocks, axis=0)]
  transfers between devices with their start and end apart: 10 -> 28, of which waited for: 7 -> 16; matrix products, arithmetic and copies ran while one was open for 11% -> 5% of each run, Pallas kernels for 0% -> 12%
where the time goes in v1:
time: 158 us
  waiting for transfers between devices  63.1 us (40%)
  starting transfers between devices  53.3 us (34%)
  Pallas kernels  30.1 us (19%)
  other arithmetic  8.65 us (5%)
  local copies, waits for them, and re-layouts  1.61 us (1%)
    ppermute x12, waiting for transfers between devices, round_x(): return lax.ppermute(a, ('core', 'x'), pairs)  38.7 us
    ppermute x12, starting transfers between devices, round_x(): return lax.ppermute(a, ('core', 'x'), pairs)  18.9 us
    ppermute x6, starting transfers between devices, across(): return lax.ppermute(a, ('core', 'y_lo'), [(1, 2), (2, 1)])  16.4 us
    ppermute x6, waiting for transfers between devices, across(): return lax.ppermute(a, ('core', 'y_lo'), [(1, 2), (2, 1)])  13.3 us
    ppermute x2, waiting for transfers between devices, next_door(): lax.ppermute(a, ('z', 'y_hi', 'y_lo'), pairs + [(j, i) for i, j in pairs])  11.1 us
    ppermute x8, starting transfers between devices, to_other_core(): return lax.ppermute(a, 'core', [(0, 1), (1, 0)])  9.96 us
    pallas_call x2, Pallas kernels, delta_and_second(): pl.pallas_call(functools.partial(delta_kernel, frames, scale, begun, star...  9.02 us
    pallas_call x1, Pallas kernels, first_layer(): pl.pallas_call(functools.partial(first_kernel, scale), in_specs=[SMEM] +...  8.86 us
  transfers between devices with their start and end apart: 28, of which 16 were waited for; matrix products, arithmetic and copies ran while one was open for 5% of the time, Pallas kernels for 12%

profile of v1, /device:TPU:1, one launch (start us, length us, event | category | flops | bytes accessed | tf_op | source)
XLA Modules:
  0.0 157.6 jit_solution(14896104150129170261)
XLA Ops:
  0.6 4.6 %collective-permute-start = (f32[128,1024]{1,0:T(8,128)}, f32[128,1024]{1,0:T(8,128)S(1)}, u32[]{:S(2)}, u32[]{:S(2)}) collective-permute-start(f32[128,1024]{1,0:T(8,128)} %bitcast.60), channel_id=1, source_target_pairs={{1,8},{8,1},{3,10},{10,3},{5,12},{12,5},{7,14},{14,7},{17,24},{24,... | collective-permute-start | bytes 1572872 | tf_op jit(solution)/shard_map/ppermute | solution.py:245
  5.2 1.9 %collective-permute-start.2 = (f32[128,1024]{1,0:T(8,128)}, f32[128,1024]{1,0:T(8,128)S(1)}, u32[]{:S(2)}, u32[]{:S(2)}) collective-permute-start(f32[128,1024]{1,0:T(8,128)} %bitcast.62), channel_id=1, source_target_pairs={{1,8},{8,1},{3,10},{10,3},{5,12},{12,5},{7,14},{14,7},{17,24},{24,... | collective-permute-start | bytes 1572872 | tf_op jit(solution)/shard_map/ppermute | solution.py:245
  7.2 5.1 %collective-permute-done = f32[128,1024]{1,0:T(8,128)S(1)} collective-permute-done((f32[128,1024]{1,0:T(8,128)}, f32[128,1024]{1,0:T(8,128)S(1)}, u32[]{:S(2)}, u32[]{:S(2)}) %collective-permute-start) | collective-permute-done | bytes 524320 | tf_op jit(solution)/shard_map/ppermute | solution.py:245
  12.3 3.6 %collective-permute-start.1 = (f32[512,1024]{1,0:T(8,128)}, f32[512,1024]{1,0:T(8,128)}, u32[]{:S(2)}, u32[]{:S(2)}) collective-permute-start(f32[512,1024]{1,0:T(8,128)} %bitcast.58), channel_id=1, source_target_pairs={{1,8},{8,1},{3,10},{10,3},{5,12},{12,5},{7,14},{14,7},{17,24},{24,... | collective-permute-start | bytes 6291464 | tf_op jit(solution)/shard_map/ppermute | solution.py:245
  15.9 1.9 %collective-permute-start.11 = (f32[512,1024]{1,0:T(8,128)}, f32[512,1024]{1,0:T(8,128)S(1)}, u32[]{:S(2)}, u32[]{:S(2)}) collective-permute-start(f32[512,1024]{1,0:T(8,128)} %bitcast.55), channel_id=1, source_target_pairs={{1,8},{8,1},{3,10},{10,3},{5,12},{12,5},{7,14},{14,7},{17,24},{24,... | collective-permute-start | bytes 6291464 | tf_op jit(solution)/shard_map/ppermute | solution.py:245
  17.9 0.3 collective-permute-done.2
  18.2 1.1 broadcast_select_fusion.1
  19.3 2.6 %collective-permute-start.3 = (f32[128,1024]{1,0:T(8,128)S(1)}, f32[128,1024]{1,0:T(8,128)S(1)}, u32[]{:S(2)}, u32[]{:S(2)}) collective-permute-start(f32[128,1024]{1,0:T(8,128)S(1)} %broadcast_select_fusion.1), channel_id=1, source_target_pairs={{0,2},{2,4},{4,6},{6,0},{8,14},{10,8},{12,10},{14,12},{1,3},{3,5},... | collective-permute-start | bytes 1572872 | tf_op jit(solution)/shard_map/ppermute | solution.py:237
  21.9 1.1 broadcast_select_fusion
  23.0 0.6 collective-permute-start.7
  23.6 4.4 %collective-permute-done.3 = f32[128,1024]{1,0:T(8,128)S(1)} collective-permute-done((f32[128,1024]{1,0:T(8,128)S(1)}, f32[128,1024]{1,0:T(8,128)S(1)}, u32[]{:S(2)}, u32[]{:S(2)}) %collective-permute-start.3) | collective-permute-done | bytes 524320 | tf_op jit(solution)/shard_map/ppermute | solution.py:237
  28.0 3.1 %collective-permute-start.4 = (f32[128,1024]{1,0:T(8,128)S(1)}, f32[128,1024]{1,0:T(8,128)S(1)}, u32[]{:S(2)}, u32[]{:S(2)}) collective-permute-start(f32[128,1024]{1,0:T(8,128)S(1)} %collective-permute-done.3), channel_id=1, source_target_pairs={{0,2},{2,4},{4,6},{6,0},{8,14},{10,8},{12,10},{14,12},{1,3},{3,5},... | collective-permute-start | bytes 1572872 | tf_op jit(solution)/shard_map/ppermute | solution.py:237
  31.1 2.5 %collective-permute-done.7 = f32[128,1024]{1,0:T(8,128)S(1)} collective-permute-done((f32[128,1024]{1,0:T(8,128)S(1)}, f32[128,1024]{1,0:T(8,128)S(1)}, u32[]{:S(2)}, u32[]{:S(2)}) %collective-permute-start.7) | collective-permute-done | bytes 524320 | tf_op jit(solution)/shard_map/ppermute | solution.py:237
  33.6 3.1 %collective-permute-start.8 = (f32[128,1024]{1,0:T(8,128)S(1)}, f32[128,1024]{1,0:T(8,128)S(1)}, u32[]{:S(2)}, u32[]{:S(2)}) collective-permute-start(f32[128,1024]{1,0:T(8,128)S(1)} %collective-permute-done.7), channel_id=1, source_target_pairs={{0,2},{2,4},{4,6},{6,0},{8,14},{10,8},{12,10},{14,12},{1,3},{3,5},... | collective-permute-start | bytes 1572872 | tf_op jit(solution)/shard_map/ppermute | solution.py:237
  36.7 2.5 %collective-permute-done.4 = f32[128,1024]{1,0:T(8,128)S(1)} collective-permute-done((f32[128,1024]{1,0:T(8,128)S(1)}, f32[128,1024]{1,0:T(8,128)S(1)}, u32[]{:S(2)}, u32[]{:S(2)}) %collective-permute-start.4) | collective-permute-done | bytes 524320 | tf_op jit(solution)/shard_map/ppermute | solution.py:237
  39.2 3.1 %collective-permute-start.5 = (f32[128,1024]{1,0:T(8,128)S(1)}, f32[128,1024]{1,0:T(8,128)S(1)}, u32[]{:S(2)}, u32[]{:S(2)}) collective-permute-start(f32[128,1024]{1,0:T(8,128)S(1)} %collective-permute-done.4), channel_id=1, source_target_pairs={{0,2},{2,4},{4,6},{6,0},{8,14},{10,8},{12,10},{14,12},{1,3},{3,5},... | collective-permute-start | bytes 1572872 | tf_op jit(solution)/shard_map/ppermute | solution.py:237
  42.3 2.5 %collective-permute-done.8 = f32[128,1024]{1,0:T(8,128)S(1)} collective-permute-done((f32[128,1024]{1,0:T(8,128)S(1)}, f32[128,1024]{1,0:T(8,128)S(1)}, u32[]{:S(2)}, u32[]{:S(2)}) %collective-permute-start.8) | collective-permute-done | bytes 524320 | tf_op jit(solution)/shard_map/ppermute | solution.py:237
  44.8 3.1 %collective-permute-start.9 = (f32[128,1024]{1,0:T(8,128)S(1)}, f32[128,1024]{1,0:T(8,128)S(1)}, u32[]{:S(2)}, u32[]{:S(2)}) collective-permute-start(f32[128,1024]{1,0:T(8,128)S(1)} %collective-permute-done.8), channel_id=1, source_target_pairs={{0,2},{2,4},{4,6},{6,0},{8,14},{10,8},{12,10},{14,12},{1,3},{3,5},... | collective-permute-start | bytes 1572872 | tf_op jit(solution)/shard_map/ppermute | solution.py:237
  48.0 2.5 %collective-permute-done.5 = f32[128,1024]{1,0:T(8,128)S(1)} collective-permute-done((f32[128,1024]{1,0:T(8,128)S(1)}, f32[128,1024]{1,0:T(8,128)S(1)}, u32[]{:S(2)}, u32[]{:S(2)}) %collective-permute-start.5) | collective-permute-done | bytes 524320 | tf_op jit(solution)/shard_map/ppermute | solution.py:237
  50.5 1.5 pad_maximum_fusion.mine
  51.9 5.0 %collective-permute-start.6 = (f32[4,128,1024]{2,1,0:T(8,128)}, f32[4,128,1024]{2,1,0:T(8,128)}, u32[]{:S(2)}, u32[]{:S(2)}) collective-permute-start(f32[4,128,1024]{2,1,0:T(8,128)} %pad_maximum_fusion.mine), channel_id=1, source_target_pairs={{0,8},{8,0},{1,9},{9,1},{2,10},{10,2},{3,11},{11,3},{4,12},{12,4},... | collective-permute-start | bytes 6291464 | tf_op jit(solution)/shard_map/ppermute | solution.py:241
  57.0 1.6 %pad_maximum_fusion.1.mine = f32[4,128,1024]{2,1,0:T(8,128)} fusion(f32[1,128,1024]{2,1,0:T(8,128)S(1)} %bitcast.70, f32[1,128,1024]{2,1,0:T(8,128)S(1)} %bitcast.68, f32[1,128,1024]{2,1,0:T(8,128)S(1)} %bitcast.66, f32[1,128,1024]{2,1,0:T(8,128)S(1)} %bitcast.64), kind=kLoop, calls=%fused_computation.1 | loop fusion | flops 1572864 | bytes 4194304 | tf_op jit(solution)/shard_map/stack | solution.py:282
  58.5 4.0 %collective-permute-done.10 = f32[128,1024]{1,0:T(8,128)S(1)} collective-permute-done((f32[128,1024]{1,0:T(8,128)S(1)}, f32[128,1024]{1,0:T(8,128)S(1)}, u32[]{:S(2)}, u32[]{:S(2)}) %collective-permute-start.10) | collective-permute-done | bytes 524320 | tf_op jit(solution)/shard_map/ppermute | solution.py:251
  62.5 0.6 collective-permute-done.11.sent
  63.1 2.5 %collective-permute-start.12 = (f32[4,128,1024]{2,1,0:T(8,128)}, f32[4,128,1024]{2,1,0:T(8,128)}, u32[]{:S(2)}, u32[]{:S(2)}) collective-permute-start(f32[4,128,1024]{2,1,0:T(8,128)} %pad_maximum_fusion.1.mine), channel_id=1, source_target_pairs={{0,8},{8,0},{1,9},{9,1},{2,10},{10,2},{3,11},{11,3},{4,12},{12,4},... | collective-permute-start | bytes 6291464 | tf_op jit(solution)/shard_map/ppermute | solution.py:241
  65.6 0.1 pad_add_fusion.at_ref
  65.7 1.6 %copy-done.1 = f32[1,512,1024]{2,1,0:T(8,128)S(1)} copy-done((f32[1,512,1024]{2,1,0:T(8,128)S(1)}, f32[1,512,1024]{2,1,0:T(8,128)}, u32[]{:S(2)}) %copy-start.1) | copy-done | bytes 2097176
  67.3 8.9 %first_layer.1 = (bf16[512,1024]{1,0:T(8,128)(2,1)S(1)}, bf16[512,1024]{1,0:T(8,128)(2,1)S(1)}, bf16[1024,512]{1,0:T(8,128)(2,1)S(1)}, bf16[1024,512]{1,0:T(8,12...) custom-call(s32[3]{0:T(128)S(1)} %pad_add_fusion.at_ref, ...), custom_call_target="tpu_custom_call" | custom-call | flops 3221225472 | bytes 16777216 | tf_op jit(solution)/shard_map/first_layer/pallas_call | solution.py:109
  76.2 7.2 %second_layer.1 = (f32[512,1024]{1,0:T(8,128)S(1)}, bf16[1024,1024]{1,0:T(8,128)(2,1)S(1)}, bf16[1024,1024]{1,0:T(8,128)(2,1)S(1)}) custom-call(s32[3]{0:T(128)S(1)} %pad_add_fusion.at_ref, bf16[512,1024]{1,0:T(8,128)(2,1)S(1)} %get-tuple-element.38.hid_h, bf16[512,1024]{1,0:T(8,128)(2,1)S(1)} %get-tuple-element.39.hid_l, ...), custom_call_target="tpu_custom_call" | custom-call | flops 3221225472 | bytes 12582912 | tf_op jit(solution)/shard_map/second_layer/pallas_call | solution.py:140
  83.4 4.4 %delta_and_second.2 = (f32[4,128,512]{2,1,0:T(8,128)S(1)}, f32[4,128,512]{2,1,0:T(8,128)S(1)}, f32[512,1024]{1,0:T(8,128)S(1)}) custom-call(s32[3]{0:T(128)S(1)} %pad_add_fusion.at_ref, f32[512,1024]{1,0:T(8,128)S(1)} %get-tuple-element.43.out, f32[512,1024]{1,0:T(8,128)S(1)} %bitcast.56, f32[512,1024]{1,0:T(8,128)S(1)} %collective-permute-done.11.sent, ...), custom_call_target="tpu_custom_call" | custom-call | flops 3221225472 | bytes 12582912 | tf_op jit(solution)/shard_map/delta_and_second/pallas_call | solution.py:190
  87.8 0.1 collective-permute-start.13
  87.9 4.6 %delta_and_second.3 = (f32[4,128,512]{2,1,0:T(8,128)S(1)}, f32[4,128,512]{2,1,0:T(8,128)S(1)}, f32[512,1024]{1,0:T(8,128)S(1)}) custom-call(s32[3]{0:T(128)S(1)} %pad_add_fusion.at_ref, f32[512,1024]{1,0:T(8,128)S(1)} %get-tuple-element.43.out, f32[512,1024]{1,0:T(8,128)S(1)} %bitcast.57, f32[512,1024]{1,0:T(8,128)S(1)} %collective-permute-done.11.sent, ...), custom_call_target="tpu_custom_call" | custom-call | flops 3221225472 | bytes 12582912 | tf_op jit(solution)/shard_map/delta_and_second/pallas_call | solution.py:190
  92.5 0.5 collective-permute-start.14
  93.1 2.5 %grad_first.3 = (f32[4,128,512]{2,1,0:T(8,128)S(1)}, f32[4,128,512]{2,1,0:T(8,128)S(1)}) custom-call(s32[3]{0:T(128)S(1)} %pad_add_fusion.at_ref, f32[512,1024]{1,0:T(8,128)S(1)} %get-tuple-element.55.back, f32[512,1024]{1,0:T(8,128)S(1)} %get-tuple-element.56.slope, bf16[1024,512]{1,0:T(8,128)(2,1)S(1)} %get-tuple-element.57.xt_h, ...), custom_call_target="tpu_custom_call" | custom-call | flops 1610612736 | bytes 6291456 | tf_op jit(solution)/shard_map/grad_first/pallas_call | solution.py:223
  95.6 0.2 collective-permute-start.16
  95.7 0.2 fusion.7
  96.0 0.2 fusion.6
  96.3 2.5 %grad_first.2 = (f32[4,128,512]{2,1,0:T(8,128)S(1)}, f32[4,128,512]{2,1,0:T(8,128)S(1)}) custom-call(s32[3]{0:T(128)S(1)} %pad_add_fusion.at_ref, f32[512,1024]{1,0:T(8,128)S(1)} %get-tuple-element.55.back, f32[512,1024]{1,0:T(8,128)S(1)} %get-tuple-element.56.slope, bf16[1024,512]{1,0:T(8,128)(2,1)S(1)} %get-tuple-element.57.xt_h, ...), custom_call_target="tpu_custom_call" | custom-call | flops 1610612736 | bytes 6291456 | tf_op jit(solution)/shard_map/grad_first/pallas_call | solution.py:223
  98.8 0.5 collective-permute-start.15
  99.3 0.2 collective-permute-start.24
  99.5 8.1 %collective-permute-done.20 = f32[128,1024]{1,0:T(8,128)S(1)} collective-permute-done((f32[128,1024]{1,0:T(8,128)S(1)}, f32[128,1024]{1,0:T(8,128)S(1)}, u32[]{:S(2)}, u32[]{:S(2)}) %collective-permute-start.20) | collective-permute-done | bytes 524320 | tf_op jit(solution)/shard_map/ppermute | solution.py:237
  107.7 1.0 collective-permute-start.21
  108.7 0.2 fusion.4
  108.9 0.2 fusion.5
  109.2 0.1 collective-permute-start.17
  109.3 8.0 %collective-permute-start.18 = (f32[128,1024]{1,0:T(8,128)S(1)}, f32[128,1024]{1,0:T(8,128)S(1)}, u32[]{:S(2)}, u32[]{:S(2)}) collective-permute-start(f32[128,1024]{1,0:T(8,128)S(1)} %broadcast_select_fusion), channel_id=1, source_target_pairs={{1,16},{17,32},{33,48},{49,64},{65,80},{81,96},{97,112},{113,128},... | collective-permute-start | bytes 1572872 | tf_op jit(solution)/shard_map/ppermute | solution.py:251
  117.3 1.0 collective-permute-start.23
  118.3 0.1 maximum_add_fusion.3
  118.3 1.6 collective-permute-start.22
  119.9 0.1 add_multiply_fusion
  120.0 1.7 %collective-permute-done.17 = f32[128,1024]{1,0:T(8,128)S(1)} collective-permute-done((f32[128,1024]{1,0:T(8,128)S(1)}, f32[128,1024]{1,0:T(8,128)S(1)}, u32[]{:S(2)}, u32[]{:S(2)}) %collective-permute-start.17) | collective-permute-done | bytes 524320 | tf_op jit(solution)/shard_map/ppermute | solution.py:237
  121.8 7.2 %collective-permute-done.18 = f32[128,1024]{1,0:T(8,128)S(1)} collective-permute-done((f32[128,1024]{1,0:T(8,128)S(1)}, f32[128,1024]{1,0:T(8,128)S(1)}, u32[]{:S(2)}, u32[]{:S(2)}) %collective-permute-start.18) | collective-permute-done | bytes 524320 | tf_op jit(solution)/shard_map/ppermute | solution.py:251
  128.9 0.1 add_multiply_fusion.1
  129.0 0.1 fusion.1
  129.2 8.5 %collective-permute-done.19 = f32[128,1024]{1,0:T(8,128)S(1)} collective-permute-done((f32[128,1024]{1,0:T(8,128)S(1)}, f32[128,1024]{1,0:T(8,128)S(1)}, u32[]{:S(2)}, u32[]{:S(2)}) %collective-permute-start.19) | collective-permute-done | bytes 524320 | tf_op jit(solution)/shard_map/ppermute | solution.py:237
  137.7 0.6 collective-permute-start.25
  138.3 1.9 %collective-permute-start.27 = (f32[128,1024]{1,0:T(8,128)S(1)}, f32[128,1024]{1,0:T(8,128)S(1)}, u32[]{:S(2)}, u32[]{:S(2)}) collective-permute-start(f32[128,1024]{1,0:T(8,128)S(1)} %fusion.1), channel_id=1, source_target_pairs={{1,8},{8,1},{3,10},{10,3},{5,12},{12,5},{7,14},{14,7},{17,24},{24,... | collective-permute-start | bytes 1572872 | tf_op jit(solution)/shard_map/ppermute | solution.py:245
  140.2 5.9 %collective-permute-done.25 = f32[128,1024]{1,0:T(8,128)S(1)} collective-permute-done((f32[128,1024]{1,0:T(8,128)S(1)}, f32[128,1024]{1,0:T(8,128)S(1)}, u32[]{:S(2)}, u32[]{:S(2)}) %collective-permute-start.25) | collective-permute-done | bytes 524320 | tf_op jit(solution)/shard_map/ppermute | solution.py:237
  146.1 0.1 fusion.3
  146.2 2.4 %collective-permute-start.26 = (f32[128,1024]{1,0:T(8,128)S(1)}, f32[128,1024]{1,0:T(8,128)S(1)}, u32[]{:S(2)}, u32[]{:S(2)}) collective-permute-start(f32[128,1024]{1,0:T(8,128)S(1)} %fusion.3), channel_id=1, source_target_pairs={{1,8},{8,1},{3,10},{10,3},{5,12},{12,5},{7,14},{14,7},{17,24},{24,... | collective-permute-start | bytes 1572872 | tf_op jit(solution)/shard_map/ppermute | solution.py:245
  148.6 0.5 collective-permute-done.27
  149.1 0.9 add_bitcast_fusion
  150.0 6.7 %collective-permute-done.26 = f32[128,1024]{1,0:T(8,128)S(1)} collective-permute-done((f32[128,1024]{1,0:T(8,128)S(1)}, f32[128,1024]{1,0:T(8,128)S(1)}, u32[]{:S(2)}, u32[]{:S(2)}) %collective-permute-start.26) | collective-permute-done | bytes 524320 | tf_op jit(solution)/shard_map/ppermute | solution.py:245
  156.7 0.9 add_bitcast_fusion.1
  (27 shorter events, 0.3 us)
Async XLA Ops:
  0.6 11.7 %collective-permute-start = (f32[128,1024]{1,0:T(8,128)}, f32[128,1024]{1,0:T(8,128)S(1)}, u32[]{:S(2)}, u32[]{:S(2)}) collective-permute-start(f32[128,1024]{1,0:T(8,128)} %bitcast.60), channel_id=1, source_target_pairs={{1,8},{8,1},{3,10},{10,3},{5,12},{12,5},{7,14},{14,7},{17,24},{24,... | collective-permute-start | bytes 1572872 | tf_op jit(solution)/shard_map/ppermute | solution.py:245
  5.2 13.0 %collective-permute-start.2 = (f32[128,1024]{1,0:T(8,128)}, f32[128,1024]{1,0:T(8,128)S(1)}, u32[]{:S(2)}, u32[]{:S(2)}) collective-permute-start(f32[128,1024]{1,0:T(8,128)} %bitcast.62), channel_id=1, source_target_pairs={{1,8},{8,1},{3,10},{10,3},{5,12},{12,5},{7,14},{14,7},{17,24},{24,... | collective-permute-start | bytes 1572872 | tf_op jit(solution)/shard_map/ppermute | solution.py:245
  12.3 32.6 %collective-permute-start.1 = (f32[512,1024]{1,0:T(8,128)}, f32[512,1024]{1,0:T(8,128)}, u32[]{:S(2)}, u32[]{:S(2)}) collective-permute-start(f32[512,1024]{1,0:T(8,128)} %bitcast.58), channel_id=1, source_target_pairs={{1,8},{8,1},{3,10},{10,3},{5,12},{12,5},{7,14},{14,7},{17,24},{24,... | collective-permute-start | bytes 6291464 | tf_op jit(solution)/shard_map/ppermute | solution.py:245
  15.9 47.2 %collective-permute-start.11 = (f32[512,1024]{1,0:T(8,128)}, f32[512,1024]{1,0:T(8,128)S(1)}, u32[]{:S(2)}, u32[]{:S(2)}) collective-permute-start(f32[512,1024]{1,0:T(8,128)} %bitcast.55), channel_id=1, source_target_pairs={{1,8},{8,1},{3,10},{10,3},{5,12},{12,5},{7,14},{14,7},{17,24},{24,... | collective-permute-start | bytes 6291464 | tf_op jit(solution)/shard_map/ppermute | solution.py:245
  19.3 8.7 %collective-permute-start.3 = (f32[128,1024]{1,0:T(8,128)S(1)}, f32[128,1024]{1,0:T(8,128)S(1)}, u32[]{:S(2)}, u32[]{:S(2)}) collective-permute-start(f32[128,1024]{1,0:T(8,128)S(1)} %broadcast_select_fusion.1), channel_id=1, source_target_pairs={{0,2},{2,4},{4,6},{6,0},{8,14},{10,8},{12,10},{14,12},{1,3},{3,5},... | collective-permute-start | bytes 1572872 | tf_op jit(solution)/shard_map/ppermute | solution.py:237
  23.0 10.6 %collective-permute-start.7 = (f32[128,1024]{1,0:T(8,128)S(1)}, f32[128,1024]{1,0:T(8,128)S(1)}, u32[]{:S(2)}, u32[]{:S(2)}) collective-permute-start(f32[128,1024]{1,0:T(8,128)S(1)} %broadcast_select_fusion), channel_id=1, source_target_pairs={{0,2},{2,4},{4,6},{6,0},{8,14},{10,8},{12,10},{14,12},{1,3},{3,5},... | collective-permute-start | bytes 1572872 | tf_op jit(solution)/shard_map/ppermute | solution.py:237
  28.0 11.2 %collective-permute-start.4 = (f32[128,1024]{1,0:T(8,128)S(1)}, f32[128,1024]{1,0:T(8,128)S(1)}, u32[]{:S(2)}, u32[]{:S(2)}) collective-permute-start(f32[128,1024]{1,0:T(8,128)S(1)} %collective-permute-done.3), channel_id=1, source_target_pairs={{0,2},{2,4},{4,6},{6,0},{8,14},{10,8},{12,10},{14,12},{1,3},{3,5},... | collective-permute-start | bytes 1572872 | tf_op jit(solution)/shard_map/ppermute | solution.py:237
  33.6 11.2 %collective-permute-start.8 = (f32[128,1024]{1,0:T(8,128)S(1)}, f32[128,1024]{1,0:T(8,128)S(1)}, u32[]{:S(2)}, u32[]{:S(2)}) collective-permute-start(f32[128,1024]{1,0:T(8,128)S(1)} %collective-permute-done.7), channel_id=1, source_target_pairs={{0,2},{2,4},{4,6},{6,0},{8,14},{10,8},{12,10},{14,12},{1,3},{3,5},... | collective-permute-start | bytes 1572872 | tf_op jit(solution)/shard_map/ppermute | solution.py:237
  39.2 11.2 %collective-permute-start.5 = (f32[128,1024]{1,0:T(8,128)S(1)}, f32[128,1024]{1,0:T(8,128)S(1)}, u32[]{:S(2)}, u32[]{:S(2)}) collective-permute-start(f32[128,1024]{1,0:T(8,128)S(1)} %collective-permute-done.4), channel_id=1, source_target_pairs={{0,2},{2,4},{4,6},{6,0},{8,14},{10,8},{12,10},{14,12},{1,3},{3,5},... | collective-permute-start | bytes 1572872 | tf_op jit(solution)/shard_map/ppermute | solution.py:237
  44.8 12.1 %collective-permute-start.9 = (f32[128,1024]{1,0:T(8,128)S(1)}, f32[128,1024]{1,0:T(8,128)S(1)}, u32[]{:S(2)}, u32[]{:S(2)}) collective-permute-start(f32[128,1024]{1,0:T(8,128)S(1)} %collective-permute-done.8), channel_id=1, source_target_pairs={{0,2},{2,4},{4,6},{6,0},{8,14},{10,8},{12,10},{14,12},{1,3},{3,5},... | collective-permute-start | bytes 1572872 | tf_op jit(solution)/shard_map/ppermute | solution.py:237
  48.0 14.6 %collective-permute-start.10 = (f32[128,1024]{1,0:T(8,128)S(1)}, f32[128,1024]{1,0:T(8,128)S(1)}, u32[]{:S(2)}, u32[]{:S(2)}) collective-permute-start(f32[128,1024]{1,0:T(8,128)S(1)} %broadcast_select_fusion.1), channel_id=1, source_target_pairs={{1,16},{17,32},{33,48},{49,64},{65,80},{81,96},{97,112},{113,128},... | collective-permute-start | bytes 1572872 | tf_op jit(solution)/shard_map/ppermute | solution.py:251
  51.9 13.8 %collective-permute-start.6 = (f32[4,128,1024]{2,1,0:T(8,128)}, f32[4,128,1024]{2,1,0:T(8,128)}, u32[]{:S(2)}, u32[]{:S(2)}) collective-permute-start(f32[4,128,1024]{2,1,0:T(8,128)} %pad_maximum_fusion.mine), channel_id=1, source_target_pairs={{0,8},{8,0},{1,9},{9,1},{2,10},{10,2},{3,11},{11,3},{4,12},{12,4},... | collective-permute-start | bytes 6291464 | tf_op jit(solution)/shard_map/ppermute | solution.py:241
  63.1 13.0 %collective-permute-start.12 = (f32[4,128,1024]{2,1,0:T(8,128)}, f32[4,128,1024]{2,1,0:T(8,128)}, u32[]{:S(2)}, u32[]{:S(2)}) collective-permute-start(f32[4,128,1024]{2,1,0:T(8,128)} %pad_maximum_fusion.1.mine), channel_id=1, source_target_pairs={{0,8},{8,0},{1,9},{9,1},{2,10},{10,2},{3,11},{11,3},{4,12},{12,4},... | collective-permute-start | bytes 6291464 | tf_op jit(solution)/shard_map/ppermute | solution.py:241
  65.7 1.6 %copy-start.1 = (f32[1,512,1024]{2,1,0:T(8,128)S(1)}, f32[1,512,1024]{2,1,0:T(8,128)}, u32[]{:S(2)}) copy-start(f32[1,512,1024]{2,1,0:T(8,128)} %param.4) | copy-start | bytes 6291460
  76.2 7.2 %copy-start = (f32[1,512,1024]{2,1,0:T(8,128)S(1)}, f32[1,512,1024]{2,1,0:T(8,128)}, u32[]{:S(2)}) copy-start(f32[1,512,1024]{2,1,0:T(8,128)} %param.5) | copy-start | bytes 6291460
  87.8 8.0 %collective-permute-start.13 = (f32[4,128,512]{2,1,0:T(8,128)S(1)}, f32[4,128,512]{2,1,0:T(8,128)S(1)}, u32[]{:S(2)}, u32[]{:S(2)}) collective-permute-start(f32[4,128,512]{2,1,0:T(8,128)S(1)} %get-tuple-element.52), channel_id=1, source_target_pairs={{0,8},{8,0},{1,9},{9,1},{2,10},{10,2},{3,11},{11,3},{4,12},{12,4},... | collective-permute-start | bytes 3145736 | tf_op jit(solution)/shard_map/ppermute | solution.py:241
  92.5 3.4 %collective-permute-start.14 = (f32[4,128,512]{2,1,0:T(8,128)S(1)}, f32[4,128,512]{2,1,0:T(8,128)S(1)}, u32[]{:S(2)}, u32[]{:S(2)}) collective-permute-start(f32[4,128,512]{2,1,0:T(8,128)S(1)} %get-tuple-element.54), channel_id=1, source_target_pairs={{0,8},{8,0},{1,9},{9,1},{2,10},{10,2},{3,11},{11,3},{4,12},{12,4},... | collective-permute-start | bytes 3145736 | tf_op jit(solution)/shard_map/ppermute | solution.py:241
  95.6 13.1 %collective-permute-start.16 = (f32[4,128,512]{2,1,0:T(8,128)S(1)}, f32[4,128,512]{2,1,0:T(8,128)S(1)}, u32[]{:S(2)}, u32[]{:S(2)}) collective-permute-start(f32[4,128,512]{2,1,0:T(8,128)S(1)} %get-tuple-element.62), channel_id=1, source_target_pairs={{0,8},{8,0},{1,9},{9,1},{2,10},{10,2},{3,11},{11,3},{4,12},{12,4},... | collective-permute-start | bytes 3145736 | tf_op jit(solution)/shard_map/ppermute | solution.py:241
  96.2 3.1 %copy-start.2 = (f32[1,128,1024]{2,1,0:T(8,128)S(1)}, f32[1,128,1024]{2,1,0:T(8,128)}, u32[]{:S(2)}) copy-start(f32[1,128,1024]{2,1,0:T(8,128)} %param.7) | copy-start | bytes 1572868
  98.8 10.1 %collective-permute-start.15 = (f32[4,128,512]{2,1,0:T(8,128)S(1)}, f32[4,128,512]{2,1,0:T(8,128)S(1)}, u32[]{:S(2)}, u32[]{:S(2)}) collective-permute-start(f32[4,128,512]{2,1,0:T(8,128)S(1)} %get-tuple-element.60), channel_id=1, source_target_pairs={{0,8},{8,0},{1,9},{9,1},{2,10},{10,2},{3,11},{11,3},{4,12},{12,4},... | collective-permute-start | bytes 3145736 | tf_op jit(solution)/shard_map/ppermute | solution.py:241
  99.3 8.3 %collective-permute-start.20 = (f32[128,1024]{1,0:T(8,128)S(1)}, f32[128,1024]{1,0:T(8,128)S(1)}, u32[]{:S(2)}, u32[]{:S(2)}) collective-permute-start(f32[128,1024]{1,0:T(8,128)S(1)} %pad_maximum_fusion.2), channel_id=1, source_target_pairs={{0,2},{2,4},{4,6},{6,0},{8,14},{10,8},{12,10},{14,12},{1,3},{3,5},... | collective-permute-start | bytes 1572872 | tf_op jit(solution)/shard_map/ppermute | solution.py:237
  99.3 20.6 %collective-permute-start.24 = (f32[128,1024]{1,0:T(8,128)S(1)}, f32[128,1024]{1,0:T(8,128)S(1)}, u32[]{:S(2)}, u32[]{:S(2)}) collective-permute-start(f32[128,1024]{1,0:T(8,128)S(1)} %bitcast.61), channel_id=1, source_target_pairs={{0,8},{8,0},{1,9},{9,1},{2,10},{10,2},{3,11},{11,3},{4,12},{12,4},... | collective-permute-start | bytes 1572872 | tf_op jit(solution)/shard_map/ppermute | solution.py:241
  107.7 10.6 %collective-permute-start.21 = (f32[128,1024]{1,0:T(8,128)S(1)}, f32[128,1024]{1,0:T(8,128)S(1)}, u32[]{:S(2)}, u32[]{:S(2)}) collective-permute-start(f32[128,1024]{1,0:T(8,128)S(1)} %maximum_add_fusion.2), channel_id=1, source_target_pairs={{0,2},{2,4},{4,6},{6,0},{8,14},{10,8},{12,10},{14,12},{1,3},{3,5},... | collective-permute-start | bytes 1572872 | tf_op jit(solution)/shard_map/ppermute | solution.py:237
  108.9 8.4 %copy-start.3 = (f32[1,128,1024]{2,1,0:T(8,128)S(1)}, f32[1,128,1024]{2,1,0:T(8,128)}, u32[]{:S(2)}) copy-start(f32[1,128,1024]{2,1,0:T(8,128)} %param.6) | copy-start | bytes 1572868
  109.2 12.5 %collective-permute-start.17 = (f32[128,1024]{1,0:T(8,128)S(1)}, f32[128,1024]{1,0:T(8,128)S(1)}, u32[]{:S(2)}, u32[]{:S(2)}) collective-permute-start(f32[128,1024]{1,0:T(8,128)S(1)} %pad_maximum_fusion.3), channel_id=1, source_target_pairs={{0,2},{2,4},{4,6},{6,0},{8,14},{10,8},{12,10},{14,12},{1,3},{3,5},... | collective-permute-start | bytes 1572872 | tf_op jit(solution)/shard_map/ppermute | solution.py:237
  109.3 19.6 %collective-permute-start.18 = (f32[128,1024]{1,0:T(8,128)S(1)}, f32[128,1024]{1,0:T(8,128)S(1)}, u32[]{:S(2)}, u32[]{:S(2)}) collective-permute-start(f32[128,1024]{1,0:T(8,128)S(1)} %broadcast_select_fusion), channel_id=1, source_target_pairs={{1,16},{17,32},{33,48},{49,64},{65,80},{81,96},{97,112},{113,128},... | collective-permute-start | bytes 1572872 | tf_op jit(solution)/shard_map/ppermute | solution.py:251
  117.3 11.6 %collective-permute-start.23 = (f32[128,1024]{1,0:T(8,128)S(1)}, f32[128,1024]{1,0:T(8,128)S(1)}, u32[]{:S(2)}, u32[]{:S(2)}) collective-permute-start(f32[128,1024]{1,0:T(8,128)S(1)} %bitcast.63), channel_id=1, source_target_pairs={{0,8},{8,0},{1,9},{9,1},{2,10},{10,2},{3,11},{11,3},{4,12},{12,4},... | collective-permute-start | bytes 1572872 | tf_op jit(solution)/shard_map/ppermute | solution.py:241
  118.3 10.7 %collective-permute-start.22 = (f32[128,1024]{1,0:T(8,128)S(1)}, f32[128,1024]{1,0:T(8,128)S(1)}, u32[]{:S(2)}, u32[]{:S(2)}) collective-permute-start(f32[128,1024]{1,0:T(8,128)S(1)} %maximum_add_fusion.3), channel_id=1, source_target_pairs={{0,2},{2,4},{4,6},{6,0},{8,14},{10,8},{12,10},{14,12},{1,3},{3,5},... | collective-permute-start | bytes 1572872 | tf_op jit(solution)/shard_map/ppermute | solution.py:237
  128.9 8.7 %collective-permute-start.19 = (f32[128,1024]{1,0:T(8,128)S(1)}, f32[128,1024]{1,0:T(8,128)S(1)}, u32[]{:S(2)}, u32[]{:S(2)}) collective-permute-start(f32[128,1024]{1,0:T(8,128)S(1)} %maximum_add_fusion), channel_id=1, source_target_pairs={{0,2},{2,4},{4,6},{6,0},{8,14},{10,8},{12,10},{14,12},{1,3},{3,5},... | collective-permute-start | bytes 1572872 | tf_op jit(solution)/shard_map/ppermute | solution.py:237
  137.7 8.4 %collective-permute-start.25 = (f32[128,1024]{1,0:T(8,128)S(1)}, f32[128,1024]{1,0:T(8,128)S(1)}, u32[]{:S(2)}, u32[]{:S(2)}) collective-permute-start(f32[128,1024]{1,0:T(8,128)S(1)} %maximum_add_fusion.1), channel_id=1, source_target_pairs={{0,2},{2,4},{4,6},{6,0},{8,14},{10,8},{12,10},{14,12},{1,3},{3,5},... | collective-permute-start | bytes 1572872 | tf_op jit(solution)/shard_map/ppermute | solution.py:237
  138.3 10.8 %collective-permute-start.27 = (f32[128,1024]{1,0:T(8,128)S(1)}, f32[128,1024]{1,0:T(8,128)S(1)}, u32[]{:S(2)}, u32[]{:S(2)}) collective-permute-start(f32[128,1024]{1,0:T(8,128)S(1)} %fusion.1), channel_id=1, source_target_pairs={{1,8},{8,1},{3,10},{10,3},{5,12},{12,5},{7,14},{14,7},{17,24},{24,... | collective-permute-start | bytes 1572872 | tf_op jit(solution)/shard_map/ppermute | solution.py:245
  146.2 10.5 %collective-permute-start.26 = (f32[128,1024]{1,0:T(8,128)S(1)}, f32[128,1024]{1,0:T(8,128)S(1)}, u32[]{:S(2)}, u32[]{:S(2)}) collective-permute-start(f32[128,1024]{1,0:T(8,128)S(1)} %fusion.3), channel_id=1, source_target_pairs={{1,8},{8,1},{3,10},{10,3},{5,12},{12,5},{7,14},{14,7},{17,24},{24,... | collective-permute-start | bytes 1572872 | tf_op jit(solution)/shard_map/ppermute | solution.py:245

commit v2 on v1

--- a/solution.py
+++ b/solution.py
@@ -51,12 +51,14 @@
             pltpu.make_async_copy(own, into, sem).start()
 
 
-def place(at_ref, gathered, high_ref, low_ref):
+def place(at_ref, copies, gathered, high_ref, low_ref):
     x, core = at_ref[0], at_ref[1]
     way = 1 - 2 * core
     rows = gathered.shape[1]
     for number in range(8):
         step, other = number % 4, number // 4
+        if step == 0:
+            copies[other].wait()
         part = core if other == 0 else 1 - core
         chip = lax.rem(x - way * step + 4 if other == 0 else x + way * step + 4, 4)
         start = pl.multiple_of((chip * 2 + part) * rows, rows)
@@ -74,18 +76,33 @@
     return copies
 
 
-def first_kernel(scale, at_ref, own, sent, mine, theirs, *refs):
-    hid_h, hid_l, hidt_h, hidt_l, slope, xt_h, xt_l, x, xh, xl, raw, wh, wl, sem = refs
-    width = x.shape[1]
-    taken = Taken(at_ref, own.at[:, pl.ds(0, width)], sent.at[:, pl.ds(0, width)], x, sem.at[2])
-    copies = fetch_weights(mine, theirs, raw, sem)
-    taken.wait()
-    high, low = split(x[...])
-    xh[...] = high
-    xl[...] = low
-    for copy in copies:
-        copy.wait()
-    place(at_ref, raw, wh, wl)
+def frames_kernel(at_ref, own, sent, xh, xl, xt_h, xt_l, x, sem):
+    Taken(at_ref, own, sent, x, sem).wait()
+    for n in range(x.shape[1] // TILE):
+        cut = slice(n * TILE, (n + 1) * TILE)
+        high, low = split(x[:, cut])
+        xh[:, cut] = high
+        xl[:, cut] = low
+        xt_h[cut, :] = high.T
+        xt_l[cut, :] = low.T
+
+
+def split_frames(at, own, sent):
+    rows, width = own.shape
+    shapes = [(rows, width)] * 2 + [(width, rows)] * 2
+    return pl.pallas_call(
+        frames_kernel,
+        in_specs=[SMEM, HBM, HBM],
+        out_specs=[VMEM] * 4,
+        out_shape=[jax.ShapeDtypeStruct(s, BF16) for s in shapes],
+        scratch_shapes=[pltpu.VMEM((rows, width), F32), pltpu.SemaphoreType.DMA],
+        name="split_frames",
+        **params(rows * width, 6 * 2**20),
+    )(at, own, sent)
+
+
+def first_kernel(scale, at_ref, xh, xl, mine, theirs, hid_h, hid_l, hidt_h, hidt_l, slope, raw, wh, wl, sem):
+    place(at_ref, fetch_weights(mine, theirs, raw, sem), raw, wh, wl)
     for n in range(slope.shape[1] // TILE):
         cut = slice(n * TILE, (n + 1) * TILE)
         pre = dot3(xh[...], xl[...], wh[:, cut], wl[:, cut]) * scale
@@ -97,38 +114,30 @@
         hid_l[:, cut] = low
         hidt_h[cut, :] = high.T
         hidt_l[cut, :] = low.T
-        xt_h[cut, :] = xh[:, cut].T
-        xt_l[cut, :] = xl[:, cut].T
-
-
-def first_layer(at, own, sent, mine, theirs, scale):
-    rows, width = own.shape[0], 8 * mine.shape[1]
+
+
+def first_layer(at, xh, xl, mine, theirs, scale):
+    rows, width = xh.shape
     hid = mine.shape[2]
-    shapes = [((rows, hid), BF16)] * 2 + [((hid, rows), BF16)] * 2
-    shapes += [((rows, hid), F32)] + [((width, rows), BF16)] * 2
+    shapes = [((rows, hid), BF16)] * 2 + [((hid, rows), BF16)] * 2 + [((rows, hid), F32)]
     return pl.pallas_call(
         functools.partial(first_kernel, scale),
-        in_specs=[SMEM] + [HBM] * 4,
+        in_specs=[SMEM, VMEM, VMEM, HBM, HBM],
         out_specs=[VMEM] * len(shapes),
         out_shape=[jax.ShapeDtypeStruct(*s) for s in shapes],
         scratch_shapes=[
-            pltpu.VMEM((rows, width), F32),
-            pltpu.VMEM((rows, width), BF16),
-            pltpu.VMEM((rows, width), BF16),
             pltpu.VMEM((8,) + mine.shape[1:], F32),
             pltpu.VMEM((width, hid), BF16),
             pltpu.VMEM((width, hid), BF16),
-            pltpu.SemaphoreType.DMA((3,)),
+            pltpu.SemaphoreType.DMA((2,)),
         ],
         name="first_layer",
         **params(6 * rows * width * hid, 16 * 2**20),
-    )(at, own, sent, mine, theirs)
+    )(at, xh, xl, mine, theirs)
 
 
 def second_kernel(scale, at_ref, hid_h, hid_l, mine, theirs, out, wh, wl, raw, sem):
-    for copy in fetch_weights(mine, theirs, raw, sem):
-        copy.wait()
-    place(at_ref, raw, wh, wl)
+    place(at_ref, fetch_weights(mine, theirs, raw, sem), raw, wh, wl)
     for n in range(out.shape[1] // TILE):
         cut = slice(n * TILE, (n + 1) * TILE)
         out[:, cut] = dot3(hid_h[...], hid_l[...], wh[:, cut], wl[:, cut]) * scale
@@ -241,14 +250,18 @@
     return lax.ppermute(a, "core", [(0, 1), (1, 0)])
 
 
-def across(a):
-    return lax.ppermute(a, ("core", "y_lo"), [(1, 2), (2, 1)])
-
-
-def next_door(a):
-    n = lax.axis_size("z") * 4
-    pairs = [(i, (i + 1) % n) for i in range(1, n, 2)]
-    return lax.ppermute(a, ("z", "y_hi", "y_lo"), pairs + [(j, i) for i, j in pairs])
+def across(a, movers=True, stayers=False):
+    places = lax.axis_size("z") * 2
+
+    def index(place, core, y_lo):
+        return (place % places) * 4 + core * 2 + y_lo
+
+    pairs = []
+    if movers:
+        pairs += [(index(i, 0, 1), index(i, 1, 0)) for i in range(places)]
+    if stayers:
+        pairs += [(index(i, 1, 1), index(i + 1, 0, 0)) for i in range(places)]
+    return lax.ppermute(a, ("z", "y_hi", "core", "y_lo"), pairs + [(j, i) for i, j in pairs])
 
 
 def after(value, *others):
@@ -266,7 +279,7 @@
     moves = core != lax.axis_index("y_lo")
     at = jnp.stack([lax.axis_index("x"), core, moves]).astype(jnp.int32)
 
-    got_first, got_second = across(own_first), across(own_second)
+    got_first, got_second = across(own_first, True, True), across(own_second, True, True)
     ring = [jnp.where(moves, got_first, own_first)]
     ring2 = [jnp.where(moves, got_second, own_second)]
     sent = across(after(inputs, got_second))
@@ -275,16 +288,18 @@
     for _ in range(2):
         ring.append(round_x(ring[-1]))
         ring2.append(round_x(ring2[-1]))
-    far_first = next_door(ring[0])
     ring.append(round_x(ring[2]))
-    ring2.append(round_x(after(ring2[2], sent)))
+    xh, xl, xt_h, xt_l = split_frames(at, inputs, sent)
+    ring2.append(round_x(after(ring2[2], xh)))
     mine = jnp.stack(ring)
     mine2 = jnp.stack(ring2)
     theirs = to_other_core(mine)
-    mine2, far_first, sent_goal = lax.optimization_barrier((mine2, far_first, sent_goal))
+    mine2, sent_goal = lax.optimization_barrier((mine2, sent_goal))
     theirs2 = to_other_core(mine2)
 
-    hid_h, hid_l, hidt_h, hidt_l, slope, xt_h, xt_l = first_layer(at, inputs, sent, mine, theirs, scale_in)
+    hid_h, hid_l, hidt_h, hidt_l, slope = first_layer(at, xh, xl, mine, theirs, scale_in)
+    got_first, got_second = lax.optimization_barrier((got_first, got_second, hid_h))[:2]
+    passed = jnp.stack([to_other_core(got_first), to_other_core(got_second)])
     out, wh, wl = second_layer(at, hid_h, hid_l, mine2, theirs2, scale_hid)
 
     def delta(start, own, sent, back):
@@ -302,23 +317,26 @@
 
     keep0, sent0, back = delta(0, goal, sent_goal, None)
     keep1, sent1, back = delta(half, goal, sent_goal, back)
-    far_second = next_door(after(ring2[0], back))
     second = (keep0, keep1), (sent0, sent1)
     m = term(*second, 3)
-    keep2, sent2 = first(0, after(back, m))
+    keep2, sent2 = first(0, back)
     keep3, sent3 = first(half, back)
     firsts = (keep2, keep3), (sent2, sent3)
     p = term(*firsts, 3)
+    far = across(after(passed, p), False, True)
     m = round_x(m) + term(*second, 2)
     p = round_x(p) + term(*firsts, 2)
     m = round_x(m) + term(*second, 1)
-    p = round_x(after(p, far_second)) + term(*firsts, 1)
+    p = round_x(p) + term(*firsts, 1)
     m = round_x(m) + term(*second, 0)
-    update_second = far_second / 3.0 - RATE * m
+    far_first, far_second = jnp.where(moves, passed, far) / 3.0
+    update_second = far_second - RATE * m
     near_first, near_second = ((w + to_other_core(after(w, back))) / 3.0 for w in (own_first, own_second))
-    p, update_second, near_first, near_second = lax.optimization_barrier((p, update_second, near_first, near_second))
+    p, update_second, near_first, near_second, far_first = lax.optimization_barrier(
+        (p, update_second, near_first, near_second, far_first)
+    )
     p = round_x(p) + term(*firsts, 0)
-    update_first = far_first / 3.0 - RATE * p
+    update_first = far_first - RATE * p
     new = []
     for near, update in ((near_first, update_first), (near_second, update_second)):
         new.append((near + jnp.where(moves, across(update), update))[None])

time: 158 us -> 146 us (0.924)
  waiting for transfers between devices: 63.1 us -> 50.1 us
  Pallas kernels: 30.1 us -> 28.1 us
  starting transfers between devices: 53.3 us -> 55 us
    ppermute x8 -> x7, waiting for transfers between devices: 24.4 us -> 14.8 us  [across(): lax.ppermute(a, ('z', 'y_hi', 'core', 'y_lo'), pairs + [(j, i) for i, j i...]
    ppermute x8 -> x7, starting transfers between devices: 24.4 us -> 16.3 us  [across(): lax.ppermute(a, ('z', 'y_hi', 'core', 'y_lo'), pairs + [(j, i) for i, j i...]
    ppermute x12, starting transfers between devices: 18.9 us -> 25.4 us  [round_x(): return lax.ppermute(a, ('core', 'x'), pairs)]
    ppermute x12, waiting for transfers between devices: 38.7 us -> 35.3 us  [round_x(): return lax.ppermute(a, ('core', 'x'), pairs)]
    ppermute x8 -> x10, starting transfers between devices: 9.96 us -> 13.3 us  [to_other_core(): return lax.ppermute(a, 'core', [(0, 1), (1, 0)])]
    pallas_call x1, Pallas kernels: 7.17 us -> 5.05 us  [second_layer(): pl.pallas_call(functools.partial(second_kernel, scale), in_specs=[SMEM, V...]
    pallas_call x1 -> x2, Pallas kernels: 8.86 us -> 8.97 us  [the longest x1 6.11 us: first_layer(): pl.pallas_call(functools.partial(first_kernel, scale), in_specs=[SMEM, VM...]
  transfers between devices with their start and end apart: 28 -> 29, of which waited for: 16 -> 14; matrix products, arithmetic and copies ran while one was open for 5% -> 6% of each run, Pallas kernels for 12% -> 13%
where the time goes in v2:
time: 146 us; the launch traced here: 145 us
  starting transfers between devices  55 us (38%)
  waiting for transfers between devices  50.1 us (34%)
  Pallas kernels  28.1 us (19%)
  other arithmetic  8.98 us (6%)
  local copies, waits for them, and re-layouts  2.07 us (1%)
    ppermute x12, waiting for transfers between devices, round_x(): return lax.ppermute(a, ('core', 'x'), pairs)  35.3 us
    ppermute x12, starting transfers between devices, round_x(): return lax.ppermute(a, ('core', 'x'), pairs)  25.4 us
    ppermute x7, starting transfers between devices, across(): lax.ppermute(a, ('z', 'y_hi', 'core', 'y_lo'), pairs + [(j, i) for i, j i...  16.3 us
    ppermute x7, waiting for transfers between devices, across(): lax.ppermute(a, ('z', 'y_hi', 'core', 'y_lo'), pairs + [(j, i) for i, j i...  14.8 us
    ppermute x10, starting transfers between devices, to_other_core(): return lax.ppermute(a, 'core', [(0, 1), (1, 0)])  13.3 us
    pallas_call x2, Pallas kernels, delta_and_second(): pl.pallas_call(functools.partial(delta_kernel, frames, scale, begun, star...  9.03 us
    pallas_call x1, Pallas kernels, first_layer(): pl.pallas_call(functools.partial(first_kernel, scale), in_specs=[SMEM, VM...  6.11 us
    pallas_call x1, Pallas kernels, second_layer(): pl.pallas_call(functools.partial(second_kernel, scale), in_specs=[SMEM, V...  5.05 us
  transfers between devices with their start and end apart: 29, of which 14 were waited for; matrix products, arithmetic and copies ran while one was open for 6% of the time, Pallas kernels for 13%

profile of v2, /device:TPU:1, one launch (start us, length us, event | category | flops | bytes accessed | tf_op | source)
XLA Modules:
  0.0 145.2 jit_solution(4800910357242569753)
XLA Ops:
  0.6 2.8 %collective-permute-start = (f32[128,1024]{1,0:T(8,128)}, f32[128,1024]{1,0:T(8,128)}, u32[]{:S(2)}, u32[]{:S(2)}) collective-permute-start(f32[128,1024]{1,0:T(8,128)} %bitcast.68), channel_id=1, source_target_pairs={{1,8},{17,24},{33,40},{49,56},{65,72},{81,88},{97,104},{113,120},{... | collective-permute-start | bytes 1572872 | tf_op jit(solution)/shard_map/ppermute | solution.py:264
  3.4 0.1 collective-permute-start.2
  3.5 7.1 %collective-permute-done = f32[128,1024]{1,0:T(8,128)} collective-permute-done((f32[128,1024]{1,0:T(8,128)}, f32[128,1024]{1,0:T(8,128)}, u32[]{:S(2)}, u32[]{:S(2)}) %collective-permute-start) | collective-permute-done | bytes 524320 | tf_op jit(solution)/shard_map/ppermute | solution.py:264
  10.6 3.6 %collective-permute-start.1 = (f32[512,1024]{1,0:T(8,128)}, f32[512,1024]{1,0:T(8,128)}, u32[]{:S(2)}, u32[]{:S(2)}) collective-permute-start(f32[512,1024]{1,0:T(8,128)} %bitcast.66), channel_id=1, source_target_pairs={{1,8},{17,24},{33,40},{49,56},{65,72},{81,88},{97,104},{113,120},{... | collective-permute-start | bytes 6291464 | tf_op jit(solution)/shard_map/ppermute | solution.py:264
  14.2 1.9 %collective-permute-start.10 = (f32[512,1024]{1,0:T(8,128)}, f32[512,1024]{1,0:T(8,128)S(1)}, u32[]{:S(2)}, u32[]{:S(2)}) collective-permute-start(f32[512,1024]{1,0:T(8,128)} %bitcast.63), channel_id=1, source_target_pairs={{1,8},{17,24},{33,40},{49,56},{65,72},{81,88},{97,104},{113,120},{... | collective-permute-start | bytes 6291464 | tf_op jit(solution)/shard_map/ppermute | solution.py:264
  16.2 0.3 collective-permute-done.2
  16.5 1.3 broadcast_select_fusion.1
  17.8 2.6 %collective-permute-start.3 = (f32[128,1024]{1,0:T(8,128)S(1)}, f32[128,1024]{1,0:T(8,128)S(1)}, u32[]{:S(2)}, u32[]{:S(2)}) collective-permute-start(f32[128,1024]{1,0:T(8,128)S(1)} %broadcast_select_fusion.1), channel_id=1, source_target_pairs={{0,2},{2,4},{4,6},{6,0},{8,14},{10,8},{12,10},{14,12},{1,3},{3,5},... | collective-permute-start | bytes 1572872 | tf_op jit(solution)/shard_map/ppermute | solution.py:246
  20.4 1.3 broadcast_select_fusion
  21.6 0.6 collective-permute-start.7
  22.2 4.2 %collective-permute-done.3 = f32[128,1024]{1,0:T(8,128)S(1)} collective-permute-done((f32[128,1024]{1,0:T(8,128)S(1)}, f32[128,1024]{1,0:T(8,128)S(1)}, u32[]{:S(2)}, u32[]{:S(2)}) %collective-permute-start.3) | collective-permute-done | bytes 524320 | tf_op jit(solution)/shard_map/ppermute | solution.py:246
  26.5 3.1 %collective-permute-start.4 = (f32[128,1024]{1,0:T(8,128)S(1)}, f32[128,1024]{1,0:T(8,128)}, u32[]{:S(2)}, u32[]{:S(2)}) collective-permute-start(f32[128,1024]{1,0:T(8,128)S(1)} %collective-permute-done.3), channel_id=1, source_target_pairs={{0,2},{2,4},{4,6},{6,0},{8,14},{10,8},{12,10},{14,12},{1,3},{3,5},... | collective-permute-start | bytes 1572872 | tf_op jit(solution)/shard_map/ppermute | solution.py:246
  29.6 2.5 %collective-permute-done.7 = f32[128,1024]{1,0:T(8,128)} collective-permute-done((f32[128,1024]{1,0:T(8,128)S(1)}, f32[128,1024]{1,0:T(8,128)}, u32[]{:S(2)}, u32[]{:S(2)}) %collective-permute-start.7) | collective-permute-done | bytes 524320 | tf_op jit(solution)/shard_map/ppermute | solution.py:246
  32.1 3.2 %collective-permute-start.8 = (f32[128,1024]{1,0:T(8,128)}, f32[128,1024]{1,0:T(8,128)}, u32[]{:S(2)}, u32[]{:S(2)}) collective-permute-start(f32[128,1024]{1,0:T(8,128)} %collective-permute-done.7), channel_id=1, source_target_pairs={{0,2},{2,4},{4,6},{6,0},{8,14},{10,8},{12,10},{14,12},{1,3},{3,5},... | collective-permute-start | bytes 1572872 | tf_op jit(solution)/shard_map/ppermute | solution.py:246
  35.3 2.4 %collective-permute-done.4 = f32[128,1024]{1,0:T(8,128)} collective-permute-done((f32[128,1024]{1,0:T(8,128)S(1)}, f32[128,1024]{1,0:T(8,128)}, u32[]{:S(2)}, u32[]{:S(2)}) %collective-permute-start.4) | collective-permute-done | bytes 524320 | tf_op jit(solution)/shard_map/ppermute | solution.py:246
  37.7 3.2 %collective-permute-start.5 = (f32[128,1024]{1,0:T(8,128)}, f32[128,1024]{1,0:T(8,128)}, u32[]{:S(2)}, u32[]{:S(2)}) collective-permute-start(f32[128,1024]{1,0:T(8,128)} %collective-permute-done.4), channel_id=1, source_target_pairs={{0,2},{2,4},{4,6},{6,0},{8,14},{10,8},{12,10},{14,12},{1,3},{3,5},... | collective-permute-start | bytes 1572872 | tf_op jit(solution)/shard_map/ppermute | solution.py:246
  41.0 1.6 %copy-done.1 = f32[1,512,1024]{2,1,0:T(8,128)S(1)} copy-done((f32[1,512,1024]{2,1,0:T(8,128)S(1)}, f32[1,512,1024]{2,1,0:T(8,128)}, u32[]{:S(2)}) %copy-start.1) | copy-done | bytes 2097176
  42.6 2.9 %split_frames.1 = (bf16[512,1024]{1,0:T(8,128)(2,1)S(1)}, bf16[512,1024]{1,0:T(8,128)(2,1)S(1)}, bf16[1024,512]{1,0:T(8,128)(2,1)S(1)}, bf16[1024,512]{1,0:T(8,128)(2,1)S(1)}) custom-call(s32[3]{0:T(128)S(1)} %pad_add_fusion.at_ref, f32[512,1024]{1,0:T(8,128)S(1)} %bitcast.67, f32[512,1024]{1,0:T(8,128)} %collective-permute-done.1.sent), custom_call_target="tpu_custom_call" | custom-call | flops 524288 | bytes 6291456 | tf_op jit(solution)/shard_map/split_frames/pallas_call | solution.py:93
  45.5 1.1 collective-permute-start.9
  46.6 2.5 %collective-permute-done.5 = f32[128,1024]{1,0:T(8,128)} collective-permute-done((f32[128,1024]{1,0:T(8,128)}, f32[128,1024]{1,0:T(8,128)}, u32[]{:S(2)}, u32[]{:S(2)}) %collective-permute-start.5) | collective-permute-done | bytes 524320 | tf_op jit(solution)/shard_map/ppermute | solution.py:246
  49.1 1.4 pad_maximum_fusion.mine
  50.5 8.0 %collective-permute-start.6 = (f32[4,128,1024]{2,1,0:T(8,128)S(1)}, f32[4,128,1024]{2,1,0:T(8,128)S(1)}, u32[]{:S(2)}, u32[]{:S(2)}) collective-permute-start(f32[4,128,1024]{2,1,0:T(8,128)S(1)} %pad_maximum_fusion.mine), channel_id=1, source_target_pairs={{0,8},{8,0},{1,9},{9,1},{2,10},{10,2},{3,11},{11,3},{4,12},{12,4},... | collective-permute-start | bytes 6291464 | tf_op jit(solution)/shard_map/ppermute | solution.py:250
  58.5 1.4 pad_maximum_fusion.1.mine
  59.9 1.4 collective-permute-done.10.sent
  61.3 2.9 %collective-permute-start.11 = (f32[4,128,1024]{2,1,0:T(8,128)S(1)}, f32[4,128,1024]{2,1,0:T(8,128)S(1)}, u32[]{:S(2)}, u32[]{:S(2)}) collective-permute-start(f32[4,128,1024]{2,1,0:T(8,128)S(1)} %pad_maximum_fusion.1.mine), channel_id=1, source_target_pairs={{0,8},{8,0},{1,9},{9,1},{2,10},{10,2},{3,11},{11,3},{4,12},{12,4},... | collective-permute-start | bytes 6291464 | tf_op jit(solution)/shard_map/ppermute | solution.py:250
  64.2 6.1 %first_layer.1 = (bf16[512,1024]{1,0:T(8,128)(2,1)S(1)}, bf16[512,1024]{1,0:T(8,128)(2,1)S(1)}, bf16[1024,512]{1,0:T(8,128)(2,1)S(1)}, bf16[1024,512]{1,0:T(8,128)(2,1)S(1)}, f32[512,1024]{1,0:T(8,128)S(1)}) custom-call(s32[3]{0:T(128)S(1)} %pad_add_fusion.at_ref, bf16[512,1024]{1,0:T(8,128)(2,1)S(1)} %get-tuple-element.40.xh, ...), custom_call_target="tpu_custom_call" | custom-call | flops 3221225472 | bytes 16777216 | tf_op jit(solution)/shard_map/first_layer/pallas_call | solution.py:123
  70.4 5.1 %second_layer.1 = (f32[512,1024]{1,0:T(8,128)S(1)}, bf16[1024,1024]{1,0:T(8,128)(2,1)S(1)}, bf16[1024,1024]{1,0:T(8,128)(2,1)S(1)}) custom-call(s32[3]{0:T(128)S(1)} %pad_add_fusion.at_ref, bf16[512,1024]{1,0:T(8,128)(2,1)S(1)} %get-tuple-element.42.hid_h, bf16[512,1024]{1,0:T(8,128)(2,1)S(1)} %get-tuple-element.43.hid_l, ...), custom_call_target="tpu_custom_call" | custom-call | flops 3221225472 | bytes 12582912 | tf_op jit(solution)/shard_map/second_layer/pallas_call | solution.py:149
  75.4 4.4 %delta_and_second.2 = (f32[4,128,512]{2,1,0:T(8,128)S(1)}, f32[4,128,512]{2,1,0:T(8,128)S(1)}, f32[512,1024]{1,0:T(8,128)S(1)}) custom-call(s32[3]{0:T(128)S(1)} %pad_add_fusion.at_ref, f32[512,1024]{1,0:T(8,128)S(1)} %get-tuple-element.47.out, f32[512,1024]{1,0:T(8,128)S(1)} %bitcast.64, f32[512,1024]{1,0:T(8,128)S(1)} %collective-permute-done.10.sent, ...), custom_call_target="tpu_custom_call" | custom-call | flops 3221225472 | bytes 12582912 | tf_op jit(solution)/shard_map/delta_and_second/pallas_call | solution.py:199
  80.0 4.6 %delta_and_second.3 = (f32[4,128,512]{2,1,0:T(8,128)S(1)}, f32[4,128,512]{2,1,0:T(8,128)S(1)}, f32[512,1024]{1,0:T(8,128)S(1)}) custom-call(s32[3]{0:T(128)S(1)} %pad_add_fusion.at_ref, f32[512,1024]{1,0:T(8,128)S(1)} %get-tuple-element.47.out, f32[512,1024]{1,0:T(8,128)S(1)} %bitcast.65, f32[512,1024]{1,0:T(8,128)S(1)} %collective-permute-done.10.sent, ...), custom_call_target="tpu_custom_call" | custom-call | flops 3221225472 | bytes 12582912 | tf_op jit(solution)/shard_map/delta_and_second/pallas_call | solution.py:199
  84.6 0.5 collective-permute-start.20
  85.1 0.1 collective-permute-start.16
  85.2 0.4 collective-permute-start.17
  85.6 2.5 %grad_first.2 = (f32[4,128,512]{2,1,0:T(8,128)S(1)}, f32[4,128,512]{2,1,0:T(8,128)S(1)}) custom-call(s32[3]{0:T(128)S(1)} %pad_add_fusion.at_ref, f32[512,1024]{1,0:T(8,128)S(1)} %get-tuple-element.54.back, f32[512,1024]{1,0:T(8,128)S(1)} %get-tuple-element.55.slope, bf16[1024,512]{1,0:T(8,128)(2,1)S(1)} %get-tuple-element.56.xt_h, ...), custom_call_target="tpu_custom_call" | custom-call | flops 1610612736 | bytes 6291456 | tf_op jit(solution)/shard_map/grad_first/pallas_call | solution.py:232
  88.2 0.2 collective-permute-start.12
  88.3 2.5 %grad_first.3 = (f32[4,128,512]{2,1,0:T(8,128)S(1)}, f32[4,128,512]{2,1,0:T(8,128)S(1)}) custom-call(s32[3]{0:T(128)S(1)} %pad_add_fusion.at_ref, f32[512,1024]{1,0:T(8,128)S(1)} %get-tuple-element.54.back, f32[512,1024]{1,0:T(8,128)S(1)} %get-tuple-element.55.slope, bf16[1024,512]{1,0:T(8,128)(2,1)S(1)} %get-tuple-element.56.xt_h, ...), custom_call_target="tpu_custom_call" | custom-call | flops 1610612736 | bytes 6291456 | tf_op jit(solution)/shard_map/grad_first/pallas_call | solution.py:232
  90.9 0.5 collective-permute-start.13
  91.5 0.4 copy-done.2
  91.9 0.4 collective-permute-start.25
  92.3 0.2 collective-permute-start.24
  92.5 0.2 fusion.7
  92.7 0.2 fusion.6
  93.0 1.3 collective-permute-start.21
  94.3 0.2 fusion.5
  94.5 0.2 fusion.4
  94.8 0.6 collective-permute-start.14
  95.4 1.0 collective-permute-start.18
  96.4 5.0 %collective-permute-done.21 = f32[128,1024]{1,0:T(8,128)S(1)} collective-permute-done((f32[128,1024]{1,0:T(8,128)S(1)}, f32[128,1024]{1,0:T(8,128)S(1)}, u32[]{:S(2)}, u32[]{:S(2)}) %collective-permute-start.21) | collective-permute-done | bytes 524320 | tf_op jit(solution)/shard_map/ppermute | solution.py:246
  101.4 2.3 %collective-permute-start.22 = (f32[128,1024]{1,0:T(8,128)S(1)}, f32[128,1024]{1,0:T(8,128)S(1)}, u32[]{:S(2)}, u32[]{:S(2)}) collective-permute-start(f32[128,1024]{1,0:T(8,128)S(1)} %maximum_add_fusion.2), channel_id=1, source_target_pairs={{0,2},{2,4},{4,6},{6,0},{8,14},{10,8},{12,10},{14,12},{1,3},{3,5},... | collective-permute-start | bytes 1572872 | tf_op jit(solution)/shard_map/ppermute | solution.py:246
  103.9 3.1 %collective-permute-done.14 = f32[128,1024]{1,0:T(8,128)S(1)} collective-permute-done((f32[128,1024]{1,0:T(8,128)S(1)}, f32[128,1024]{1,0:T(8,128)S(1)}, u32[]{:S(2)}, u32[]{:S(2)}) %collective-permute-start.14) | collective-permute-done | bytes 524320 | tf_op jit(solution)/shard_map/ppermute | solution.py:246
  107.0 2.6 %collective-permute-start.15 = (f32[128,1024]{1,0:T(8,128)S(1)}, f32[128,1024]{1,0:T(8,128)S(1)}, u32[]{:S(2)}, u32[]{:S(2)}) collective-permute-start(f32[128,1024]{1,0:T(8,128)S(1)} %maximum_add_fusion), channel_id=1, source_target_pairs={{0,2},{2,4},{4,6},{6,0},{8,14},{10,8},{12,10},{14,12},{1,3},{3,5},... | collective-permute-start | bytes 1572872 | tf_op jit(solution)/shard_map/ppermute | solution.py:246
  109.6 3.0 %collective-permute-done.22 = f32[128,1024]{1,0:T(8,128)S(1)} collective-permute-done((f32[128,1024]{1,0:T(8,128)S(1)}, f32[128,1024]{1,0:T(8,128)S(1)}, u32[]{:S(2)}, u32[]{:S(2)}) %collective-permute-start.22) | collective-permute-done | bytes 524320 | tf_op jit(solution)/shard_map/ppermute | solution.py:246
  112.7 2.6 %collective-permute-start.23 = (f32[128,1024]{1,0:T(8,128)S(1)}, f32[128,1024]{1,0:T(8,128)S(1)}, u32[]{:S(2)}, u32[]{:S(2)}) collective-permute-start(f32[128,1024]{1,0:T(8,128)S(1)} %maximum_add_fusion.3), channel_id=1, source_target_pairs={{0,2},{2,4},{4,6},{6,0},{8,14},{10,8},{12,10},{14,12},{1,3},{3,5},... | collective-permute-start | bytes 1572872 | tf_op jit(solution)/shard_map/ppermute | solution.py:246
  115.2 0.2 select_multiply_fusion
  115.4 2.8 %collective-permute-done.15 = f32[128,1024]{1,0:T(8,128)S(1)} collective-permute-done((f32[128,1024]{1,0:T(8,128)S(1)}, f32[128,1024]{1,0:T(8,128)S(1)}, u32[]{:S(2)}, u32[]{:S(2)}) %collective-permute-start.15) | collective-permute-done | bytes 524320 | tf_op jit(solution)/shard_map/ppermute | solution.py:246
  118.3 5.6 %collective-permute-done.23 = f32[128,1024]{1,0:T(8,128)S(1)} collective-permute-done((f32[128,1024]{1,0:T(8,128)S(1)}, f32[128,1024]{1,0:T(8,128)S(1)}, u32[]{:S(2)}, u32[]{:S(2)}) %collective-permute-start.23) | collective-permute-done | bytes 524320 | tf_op jit(solution)/shard_map/ppermute | solution.py:246
  123.8 0.1 fusion
  124.0 2.3 %collective-permute-start.26 = (f32[128,1024]{1,0:T(8,128)S(1)}, f32[128,1024]{1,0:T(8,128)S(1)}, u32[]{:S(2)}, u32[]{:S(2)}) collective-permute-start(f32[128,1024]{1,0:T(8,128)S(1)} %maximum_add_fusion.1), channel_id=1, source_target_pairs={{0,2},{2,4},{4,6},{6,0},{8,14},{10,8},{12,10},{14,12},{1,3},{3,5},... | collective-permute-start | bytes 1572872 | tf_op jit(solution)/shard_map/ppermute | solution.py:246
  126.2 1.9 %collective-permute-start.28 = (f32[128,1024]{1,0:T(8,128)S(1)}, f32[128,1024]{1,0:T(8,128)S(1)}, u32[]{:S(2)}, u32[]{:S(2)}) collective-permute-start(f32[128,1024]{1,0:T(8,128)S(1)} %fusion), channel_id=1, source_target_pairs={{1,8},{17,24},{33,40},{49,56},{65,72},{81,88},{97,104},{113,120},{... | collective-permute-start | bytes 1572872 | tf_op jit(solution)/shard_map/ppermute | solution.py:264
  128.1 4.2 %collective-permute-done.26 = f32[128,1024]{1,0:T(8,128)S(1)} collective-permute-done((f32[128,1024]{1,0:T(8,128)S(1)}, f32[128,1024]{1,0:T(8,128)S(1)}, u32[]{:S(2)}, u32[]{:S(2)}) %collective-permute-start.26) | collective-permute-done | bytes 524320 | tf_op jit(solution)/shard_map/ppermute | solution.py:246
  132.4 0.1 fusion.3
  132.5 5.0 %collective-permute-start.27 = (f32[128,1024]{1,0:T(8,128)S(1)}, f32[128,1024]{1,0:T(8,128)S(1)}, u32[]{:S(2)}, u32[]{:S(2)}) collective-permute-start(f32[128,1024]{1,0:T(8,128)S(1)} %fusion.3), channel_id=1, source_target_pairs={{1,8},{17,24},{33,40},{49,56},{65,72},{81,88},{97,104},{113,120},{... | collective-permute-start | bytes 1572872 | tf_op jit(solution)/shard_map/ppermute | solution.py:264
  137.5 0.9 add_bitcast_fusion
  138.4 6.0 %collective-permute-done.27 = f32[128,1024]{1,0:T(8,128)S(1)} collective-permute-done((f32[128,1024]{1,0:T(8,128)S(1)}, f32[128,1024]{1,0:T(8,128)S(1)}, u32[]{:S(2)}, u32[]{:S(2)}) %collective-permute-start.27) | collective-permute-done | bytes 524320 | tf_op jit(solution)/shard_map/ppermute | solution.py:264
  144.3 0.9 add_bitcast_fusion.1
  (41 shorter events, 0.8 us)
Async XLA Ops:
  0.6 10.0 %collective-permute-start = (f32[128,1024]{1,0:T(8,128)}, f32[128,1024]{1,0:T(8,128)}, u32[]{:S(2)}, u32[]{:S(2)}) collective-permute-start(f32[128,1024]{1,0:T(8,128)} %bitcast.68), channel_id=1, source_target_pairs={{1,8},{17,24},{33,40},{49,56},{65,72},{81,88},{97,104},{113,120},{... | collective-permute-start | bytes 1572872 | tf_op jit(solution)/shard_map/ppermute | solution.py:264
  3.4 13.1 %collective-permute-start.2 = (f32[128,1024]{1,0:T(8,128)}, f32[128,1024]{1,0:T(8,128)S(1)}, u32[]{:S(2)}, u32[]{:S(2)}) collective-permute-start(f32[128,1024]{1,0:T(8,128)} %bitcast.70), channel_id=1, source_target_pairs={{1,8},{17,24},{33,40},{49,56},{65,72},{81,88},{97,104},{113,120},{... | collective-permute-start | bytes 1572872 | tf_op jit(solution)/shard_map/ppermute | solution.py:264
  10.6 30.4 %collective-permute-start.1 = (f32[512,1024]{1,0:T(8,128)}, f32[512,1024]{1,0:T(8,128)}, u32[]{:S(2)}, u32[]{:S(2)}) collective-permute-start(f32[512,1024]{1,0:T(8,128)} %bitcast.66), channel_id=1, source_target_pairs={{1,8},{17,24},{33,40},{49,56},{65,72},{81,88},{97,104},{113,120},{... | collective-permute-start | bytes 6291464 | tf_op jit(solution)/shard_map/ppermute | solution.py:264
  14.2 47.1 %collective-permute-start.10 = (f32[512,1024]{1,0:T(8,128)}, f32[512,1024]{1,0:T(8,128)S(1)}, u32[]{:S(2)}, u32[]{:S(2)}) collective-permute-start(f32[512,1024]{1,0:T(8,128)} %bitcast.63), channel_id=1, source_target_pairs={{1,8},{17,24},{33,40},{49,56},{65,72},{81,88},{97,104},{113,120},{... | collective-permute-start | bytes 6291464 | tf_op jit(solution)/shard_map/ppermute | solution.py:264
  16.5 1.3 copy-start.4
  17.8 8.7 %collective-permute-start.3 = (f32[128,1024]{1,0:T(8,128)S(1)}, f32[128,1024]{1,0:T(8,128)S(1)}, u32[]{:S(2)}, u32[]{:S(2)}) collective-permute-start(f32[128,1024]{1,0:T(8,128)S(1)} %broadcast_select_fusion.1), channel_id=1, source_target_pairs={{0,2},{2,4},{4,6},{6,0},{8,14},{10,8},{12,10},{14,12},{1,3},{3,5},... | collective-permute-start | bytes 1572872 | tf_op jit(solution)/shard_map/ppermute | solution.py:246
  21.6 10.5 %collective-permute-start.7 = (f32[128,1024]{1,0:T(8,128)S(1)}, f32[128,1024]{1,0:T(8,128)}, u32[]{:S(2)}, u32[]{:S(2)}) collective-permute-start(f32[128,1024]{1,0:T(8,128)S(1)} %broadcast_select_fusion), channel_id=1, source_target_pairs={{0,2},{2,4},{4,6},{6,0},{8,14},{10,8},{12,10},{14,12},{1,3},{3,5},... | collective-permute-start | bytes 1572872 | tf_op jit(solution)/shard_map/ppermute | solution.py:246
  26.5 5.6 %copy-start.6 = (f32[128,1024]{1,0:T(8,128)}, f32[128,1024]{1,0:T(8,128)S(1)}, u32[]{:S(2)}) copy-start(f32[128,1024]{1,0:T(8,128)S(1)} %collective-permute-done.3) | copy-start | bytes 1572868
  26.5 11.2 %collective-permute-start.4 = (f32[128,1024]{1,0:T(8,128)S(1)}, f32[128,1024]{1,0:T(8,128)}, u32[]{:S(2)}, u32[]{:S(2)}) collective-permute-start(f32[128,1024]{1,0:T(8,128)S(1)} %collective-permute-done.3), channel_id=1, source_target_pairs={{0,2},{2,4},{4,6},{6,0},{8,14},{10,8},{12,10},{14,12},{1,3},{3,5},... | collective-permute-start | bytes 1572872 | tf_op jit(solution)/shard_map/ppermute | solution.py:246
  32.1 13.4 %collective-permute-start.8 = (f32[128,1024]{1,0:T(8,128)}, f32[128,1024]{1,0:T(8,128)}, u32[]{:S(2)}, u32[]{:S(2)}) collective-permute-start(f32[128,1024]{1,0:T(8,128)} %collective-permute-done.7), channel_id=1, source_target_pairs={{0,2},{2,4},{4,6},{6,0},{8,14},{10,8},{12,10},{14,12},{1,3},{3,5},... | collective-permute-start | bytes 1572872 | tf_op jit(solution)/shard_map/ppermute | solution.py:246
  37.7 11.3 %collective-permute-start.5 = (f32[128,1024]{1,0:T(8,128)}, f32[128,1024]{1,0:T(8,128)}, u32[]{:S(2)}, u32[]{:S(2)}) collective-permute-start(f32[128,1024]{1,0:T(8,128)} %collective-permute-done.4), channel_id=1, source_target_pairs={{0,2},{2,4},{4,6},{6,0},{8,14},{10,8},{12,10},{14,12},{1,3},{3,5},... | collective-permute-start | bytes 1572872 | tf_op jit(solution)/shard_map/ppermute | solution.py:246
  41.0 1.6 %copy-start.1 = (f32[1,512,1024]{2,1,0:T(8,128)S(1)}, f32[1,512,1024]{2,1,0:T(8,128)}, u32[]{:S(2)}) copy-start(f32[1,512,1024]{2,1,0:T(8,128)} %param.4) | copy-start | bytes 6291460
  42.6 6.4 %copy-start.7 = (f32[128,1024]{1,0:T(8,128)S(1)}, f32[128,1024]{1,0:T(8,128)}, u32[]{:S(2)}) copy-start(f32[128,1024]{1,0:T(8,128)} %copy-done.6) | copy-start | bytes 1572868
  45.5 13.0 %collective-permute-start.9 = (f32[128,1024]{1,0:T(8,128)}, f32[128,1024]{1,0:T(8,128)S(1)}, u32[]{:S(2)}, u32[]{:S(2)}) collective-permute-start(f32[128,1024]{1,0:T(8,128)} %collective-permute-done.8), channel_id=1, source_target_pairs={{0,2},{2,4},{4,6},{6,0},{8,14},{10,8},{12,10},{14,12},{1,3},{3,5},... | collective-permute-start | bytes 1572872 | tf_op jit(solution)/shard_map/ppermute | solution.py:246
  50.5 13.8 %collective-permute-start.6 = (f32[4,128,1024]{2,1,0:T(8,128)S(1)}, f32[4,128,1024]{2,1,0:T(8,128)S(1)}, u32[]{:S(2)}, u32[]{:S(2)}) collective-permute-start(f32[4,128,1024]{2,1,0:T(8,128)S(1)} %pad_maximum_fusion.mine), channel_id=1, source_target_pairs={{0,8},{8,0},{1,9},{9,1},{2,10},{10,2},{3,11},{11,3},{4,12},{12,4},... | collective-permute-start | bytes 6291464 | tf_op jit(solution)/shard_map/ppermute | solution.py:250
  61.3 9.0 %collective-permute-start.11 = (f32[4,128,1024]{2,1,0:T(8,128)S(1)}, f32[4,128,1024]{2,1,0:T(8,128)S(1)}, u32[]{:S(2)}, u32[]{:S(2)}) collective-permute-start(f32[4,128,1024]{2,1,0:T(8,128)S(1)} %pad_maximum_fusion.1.mine), channel_id=1, source_target_pairs={{0,8},{8,0},{1,9},{9,1},{2,10},{10,2},{3,11},{11,3},{4,12},{12,4},... | collective-permute-start | bytes 6291464 | tf_op jit(solution)/shard_map/ppermute | solution.py:250
  70.4 5.1 %copy-start = (f32[1,512,1024]{2,1,0:T(8,128)S(1)}, f32[1,512,1024]{2,1,0:T(8,128)}, u32[]{:S(2)}) copy-start(f32[1,512,1024]{2,1,0:T(8,128)} %param.5) | copy-start | bytes 6291460
  79.8 12.5 %collective-permute-start.19 = (f32[4,128,512]{2,1,0:T(8,128)S(1)}, f32[4,128,512]{2,1,0:T(8,128)S(1)}, u32[]{:S(2)}, u32[]{:S(2)}) collective-permute-start(f32[4,128,512]{2,1,0:T(8,128)S(1)} %get-tuple-element.66), channel_id=1, source_target_pairs={{0,8},{8,0},{1,9},{9,1},{2,10},{10,2},{3,11},{11,3},{4,12},{12,4},... | collective-permute-start | bytes 3145736 | tf_op jit(solution)/shard_map/ppermute | solution.py:250
  79.9 5.2 %copy-start.5 = (f32[128,1024]{1,0:T(8,128)S(1)}, f32[128,1024]{1,0:T(8,128)}, u32[]{:S(2)}) copy-start(f32[128,1024]{1,0:T(8,128)} %copy-done.4) | copy-start | bytes 1572868
  84.6 8.1 %collective-permute-start.20 = (f32[4,128,512]{2,1,0:T(8,128)S(1)}, f32[4,128,512]{2,1,0:T(8,128)S(1)}, u32[]{:S(2)}, u32[]{:S(2)}) collective-permute-start(f32[4,128,512]{2,1,0:T(8,128)S(1)} %get-tuple-element.68), channel_id=1, source_target_pairs={{0,8},{8,0},{1,9},{9,1},{2,10},{10,2},{3,11},{11,3},{4,12},{12,4},... | collective-permute-start | bytes 3145736 | tf_op jit(solution)/shard_map/ppermute | solution.py:250
  85.1 5.8 %collective-permute-start.16 = (f32[128,1024]{1,0:T(8,128)S(1)}, f32[128,1024]{1,0:T(8,128)S(1)}, u32[]{:S(2)}, u32[]{:S(2)}) collective-permute-start(f32[128,1024]{1,0:T(8,128)S(1)} %copy-done.5), channel_id=1, source_target_pairs={{0,8},{8,0},{1,9},{9,1},{2,10},{10,2},{3,11},{11,3},{4,12},{12,4},... | collective-permute-start | bytes 1572872 | tf_op jit(solution)/shard_map/ppermute | solution.py:250
  85.2 6.2 %collective-permute-start.17 = (f32[128,1024]{1,0:T(8,128)}, f32[128,1024]{1,0:T(8,128)S(1)}, u32[]{:S(2)}, u32[]{:S(2)}) collective-permute-start(f32[128,1024]{1,0:T(8,128)} %collective-permute-done), channel_id=1, source_target_pairs={{0,8},{8,0},{1,9},{9,1},{2,10},{10,2},{3,11},{11,3},{4,12},{12,4},... | collective-permute-start | bytes 1572872 | tf_op jit(solution)/shard_map/ppermute | solution.py:250
  88.2 6.2 %collective-permute-start.12 = (f32[4,128,512]{2,1,0:T(8,128)S(1)}, f32[4,128,512]{2,1,0:T(8,128)S(1)}, u32[]{:S(2)}, u32[]{:S(2)}) collective-permute-start(f32[4,128,512]{2,1,0:T(8,128)S(1)} %get-tuple-element.59), channel_id=1, source_target_pairs={{0,8},{8,0},{1,9},{9,1},{2,10},{10,2},{3,11},{11,3},{4,12},{12,4},... | collective-permute-start | bytes 3145736 | tf_op jit(solution)/shard_map/ppermute | solution.py:250
  90.9 1.0 copy-start.2
  90.9 1.4 copy-start.3
  90.9 3.6 %collective-permute-start.13 = (f32[4,128,512]{2,1,0:T(8,128)S(1)}, f32[4,128,512]{2,1,0:T(8,128)S(1)}, u32[]{:S(2)}, u32[]{:S(2)}) collective-permute-start(f32[4,128,512]{2,1,0:T(8,128)S(1)} %get-tuple-element.61), channel_id=1, source_target_pairs={{0,8},{8,0},{1,9},{9,1},{2,10},{10,2},{3,11},{11,3},{4,12},{12,4},... | collective-permute-start | bytes 3145736 | tf_op jit(solution)/shard_map/ppermute | solution.py:250
  91.9 11.8 %collective-permute-start.25 = (f32[128,1024]{1,0:T(8,128)S(1)}, f32[128,1024]{1,0:T(8,128)S(1)}, u32[]{:S(2)}, u32[]{:S(2)}) collective-permute-start(f32[128,1024]{1,0:T(8,128)S(1)} %bitcast.69), channel_id=1, source_target_pairs={{0,8},{8,0},{1,9},{9,1},{2,10},{10,2},{3,11},{11,3},{4,12},{12,4},... | collective-permute-start | bytes 1572872 | tf_op jit(solution)/shard_map/ppermute | solution.py:250
  92.3 11.5 %collective-permute-start.24 = (f32[128,1024]{1,0:T(8,128)S(1)}, f32[128,1024]{1,0:T(8,128)S(1)}, u32[]{:S(2)}, u32[]{:S(2)}) collective-permute-start(f32[128,1024]{1,0:T(8,128)S(1)} %bitcast.71), channel_id=1, source_target_pairs={{0,8},{8,0},{1,9},{9,1},{2,10},{10,2},{3,11},{11,3},{4,12},{12,4},... | collective-permute-start | bytes 1572872 | tf_op jit(solution)/shard_map/ppermute | solution.py:250
  93.0 8.4 %collective-permute-start.21 = (f32[128,1024]{1,0:T(8,128)S(1)}, f32[128,1024]{1,0:T(8,128)S(1)}, u32[]{:S(2)}, u32[]{:S(2)}) collective-permute-start(f32[128,1024]{1,0:T(8,128)S(1)} %pad_maximum_fusion.4), channel_id=1, source_target_pairs={{0,2},{2,4},{4,6},{6,0},{8,14},{10,8},{12,10},{14,12},{1,3},{3,5},... | collective-permute-start | bytes 1572872 | tf_op jit(solution)/shard_map/ppermute | solution.py:246
  94.8 12.2 %collective-permute-start.14 = (f32[128,1024]{1,0:T(8,128)S(1)}, f32[128,1024]{1,0:T(8,128)S(1)}, u32[]{:S(2)}, u32[]{:S(2)}) collective-permute-start(f32[128,1024]{1,0:T(8,128)S(1)} %pad_maximum_fusion.3), channel_id=1, source_target_pairs={{0,2},{2,4},{4,6},{6,0},{8,14},{10,8},{12,10},{14,12},{1,3},{3,5},... | collective-permute-start | bytes 1572872 | tf_op jit(solution)/shard_map/ppermute | solution.py:246
  95.4 19.8 %collective-permute-start.18 = (f32[2,128,1024]{2,1,0:T(8,128)S(1)}, f32[2,128,1024]{2,1,0:T(8,128)S(1)}, u32[]{:S(2)}, u32[]{:S(2)}) collective-permute-start(f32[2,128,1024]{2,1,0:T(8,128)S(1)} %pad_maximum_fusion.2), channel_id=1, source_target_pairs={{9,16},{25,32},{41,48},{57,64},{73,80},{89,96},{105,112},{121,128}... | collective-permute-start | bytes 3145736 | tf_op jit(solution)/shard_map/ppermute | solution.py:264
  101.4 11.2 %collective-permute-start.22 = (f32[128,1024]{1,0:T(8,128)S(1)}, f32[128,1024]{1,0:T(8,128)S(1)}, u32[]{:S(2)}, u32[]{:S(2)}) collective-permute-start(f32[128,1024]{1,0:T(8,128)S(1)} %maximum_add_fusion.2), channel_id=1, source_target_pairs={{0,2},{2,4},{4,6},{6,0},{8,14},{10,8},{12,10},{14,12},{1,3},{3,5},... | collective-permute-start | bytes 1572872 | tf_op jit(solution)/shard_map/ppermute | solution.py:246
  107.0 11.2 %collective-permute-start.15 = (f32[128,1024]{1,0:T(8,128)S(1)}, f32[128,1024]{1,0:T(8,128)S(1)}, u32[]{:S(2)}, u32[]{:S(2)}) collective-permute-start(f32[128,1024]{1,0:T(8,128)S(1)} %maximum_add_fusion), channel_id=1, source_target_pairs={{0,2},{2,4},{4,6},{6,0},{8,14},{10,8},{12,10},{14,12},{1,3},{3,5},... | collective-permute-start | bytes 1572872 | tf_op jit(solution)/shard_map/ppermute | solution.py:246
  112.7 11.2 %collective-permute-start.23 = (f32[128,1024]{1,0:T(8,128)S(1)}, f32[128,1024]{1,0:T(8,128)S(1)}, u32[]{:S(2)}, u32[]{:S(2)}) collective-permute-start(f32[128,1024]{1,0:T(8,128)S(1)} %maximum_add_fusion.3), channel_id=1, source_target_pairs={{0,2},{2,4},{4,6},{6,0},{8,14},{10,8},{12,10},{14,12},{1,3},{3,5},... | collective-permute-start | bytes 1572872 | tf_op jit(solution)/shard_map/ppermute | solution.py:246
  124.0 8.4 %collective-permute-start.26 = (f32[128,1024]{1,0:T(8,128)S(1)}, f32[128,1024]{1,0:T(8,128)S(1)}, u32[]{:S(2)}, u32[]{:S(2)}) collective-permute-start(f32[128,1024]{1,0:T(8,128)S(1)} %maximum_add_fusion.1), channel_id=1, source_target_pairs={{0,2},{2,4},{4,6},{6,0},{8,14},{10,8},{12,10},{14,12},{1,3},{3,5},... | collective-permute-start | bytes 1572872 | tf_op jit(solution)/shard_map/ppermute | solution.py:246
  126.2 11.2 %collective-permute-start.28 = (f32[128,1024]{1,0:T(8,128)S(1)}, f32[128,1024]{1,0:T(8,128)S(1)}, u32[]{:S(2)}, u32[]{:S(2)}) collective-permute-start(f32[128,1024]{1,0:T(8,128)S(1)} %fusion), channel_id=1, source_target_pairs={{1,8},{17,24},{33,40},{49,56},{65,72},{81,88},{97,104},{113,120},{... | collective-permute-start | bytes 1572872 | tf_op jit(solution)/shard_map/ppermute | solution.py:264
  132.5 11.8 %collective-permute-start.27 = (f32[128,1024]{1,0:T(8,128)S(1)}, f32[128,1024]{1,0:T(8,128)S(1)}, u32[]{:S(2)}, u32[]{:S(2)}) collective-permute-start(f32[128,1024]{1,0:T(8,128)S(1)} %fusion.3), channel_id=1, source_target_pairs={{1,8},{17,24},{33,40},{49,56},{65,72},{81,88},{97,104},{113,120},{... | collective-permute-start | bytes 1572872 | tf_op jit(solution)/shard_map/ppermute | solution.py:264

commit v3 on v2

--- a/solution.py
+++ b/solution.py
@@ -309,7 +309,7 @@
         return keep, to_other_core(send), back
 
     def first(start, back):
-        keep, send = grad_first(at, start, half, back, slope, xt_h, xt_l, scale_hid, scale_in)
+        keep, send = grad_first(at, start, width, back, slope, xt_h, xt_l, scale_hid, scale_in)
         return keep, to_other_core(send)
 
     def term(keeps, sents, k):
@@ -320,8 +320,7 @@
     second = (keep0, keep1), (sent0, sent1)
     m = term(*second, 3)
     keep2, sent2 = first(0, back)
-    keep3, sent3 = first(half, back)
-    firsts = (keep2, keep3), (sent2, sent3)
+    firsts = (keep2,), (sent2,)
     p = term(*firsts, 3)
     far = across(after(passed, p), False, True)
     m = round_x(m) + term(*second, 2)

time: 146 us -> 148 us (1.014)
  starting transfers between devices: 55 us -> 57.3 us
  waiting for transfers between devices: 50.1 us -> 51.8 us
    ppermute x10 -> x9, waiting for transfers between devices: 0.03 us -> 3.4 us  [to_other_core(): return lax.ppermute(a, 'core', [(0, 1), (1, 0)])]
    ppermute x12, starting transfers between devices: 25.4 us -> 27.6 us  [round_x(): return lax.ppermute(a, ('core', 'x'), pairs)]
    ppermute x12, waiting for transfers between devices: 35.3 us -> 33.7 us  [round_x(): return lax.ppermute(a, ('core', 'x'), pairs)]
    ppermute x10 -> x9, starting transfers between devices: 13.3 us -> 12.5 us  [to_other_core(): return lax.ppermute(a, 'core', [(0, 1), (1, 0)])]
    pallas_call x2 -> x1, Pallas kernels: 5.03 us -> 4.32 us  [grad_first(): pl.pallas_call(functools.partial(grad_first_kernel, scale_hid, scale_in,...]
  transfers between devices with their start and end apart: 29 -> 28, of which waited for: 14 -> 16; matrix products, arithmetic and copies ran while one was open for 6% -> 5% of each run, Pallas kernels for 13% -> 12%
where the time goes in v3:
time: 148 us
  starting transfers between devices  57.3 us (39%)
  waiting for transfers between devices  51.8 us (35%)
  Pallas kernels  27.4 us (19%)
  other arithmetic  8.77 us (6%)
  local copies, waits for them, and re-layouts  1.67 us (1%)
    ppermute x12, waiting for transfers between devices, round_x(): return lax.ppermute(a, ('core', 'x'), pairs)  33.7 us
    ppermute x12, starting transfers between devices, round_x(): return lax.ppermute(a, ('core', 'x'), pairs)  27.6 us
    ppermute x7, starting transfers between devices, across(): lax.ppermute(a, ('z', 'y_hi', 'core', 'y_lo'), pairs + [(j, i) for i, j i...  17.2 us
    ppermute x7, waiting for transfers between devices, across(): lax.ppermute(a, ('z', 'y_hi', 'core', 'y_lo'), pairs + [(j, i) for i, j i...  14.7 us
    ppermute x9, starting transfers between devices, to_other_core(): return lax.ppermute(a, 'core', [(0, 1), (1, 0)])  12.5 us
    pallas_call x2, Pallas kernels, delta_and_second(): pl.pallas_call(functools.partial(delta_kernel, frames, scale, begun, star...  9.03 us
    pallas_call x1, Pallas kernels, first_layer(): pl.pallas_call(functools.partial(first_kernel, scale), in_specs=[SMEM, VM...  6.11 us
    pallas_call x1, Pallas kernels, second_layer(): pl.pallas_call(functools.partial(second_kernel, scale), in_specs=[SMEM, V...  5.05 us
  transfers between devices with their start and end apart: 28, of which 16 were waited for; matrix products, arithmetic and copies ran while one was open for 5% of the time, Pallas kernels for 12%

profile of v3, /device:TPU:1, one launch (start us, length us, event | category | flops | bytes accessed | tf_op | source)
XLA Modules:
  0.0 147.9 jit_solution(3601914452752963269)
XLA Ops:
  0.6 2.8 %collective-permute-start = (f32[128,1024]{1,0:T(8,128)}, f32[128,1024]{1,0:T(8,128)}, u32[]{:S(2)}, u32[]{:S(2)}) collective-permute-start(f32[128,1024]{1,0:T(8,128)} %bitcast.70), channel_id=1, source_target_pairs={{1,8},{17,24},{33,40},{49,56},{65,72},{81,88},{97,104},{113,120},{... | collective-permute-start | bytes 1572872 | tf_op jit(solution)/shard_map/ppermute | solution.py:264
  3.4 0.1 collective-permute-start.2
  3.5 7.1 %collective-permute-done = f32[128,1024]{1,0:T(8,128)} collective-permute-done((f32[128,1024]{1,0:T(8,128)}, f32[128,1024]{1,0:T(8,128)}, u32[]{:S(2)}, u32[]{:S(2)}) %collective-permute-start) | collective-permute-done | bytes 524320 | tf_op jit(solution)/shard_map/ppermute | solution.py:264
  10.6 3.6 %collective-permute-start.1 = (f32[512,1024]{1,0:T(8,128)}, f32[512,1024]{1,0:T(8,128)}, u32[]{:S(2)}, u32[]{:S(2)}) collective-permute-start(f32[512,1024]{1,0:T(8,128)} %bitcast.68), channel_id=1, source_target_pairs={{1,8},{17,24},{33,40},{49,56},{65,72},{81,88},{97,104},{113,120},{... | collective-permute-start | bytes 6291464 | tf_op jit(solution)/shard_map/ppermute | solution.py:264
  14.2 1.9 %collective-permute-start.10 = (f32[512,1024]{1,0:T(8,128)}, f32[512,1024]{1,0:T(8,128)S(1)}, u32[]{:S(2)}, u32[]{:S(2)}) collective-permute-start(f32[512,1024]{1,0:T(8,128)} %bitcast.65), channel_id=1, source_target_pairs={{1,8},{17,24},{33,40},{49,56},{65,72},{81,88},{97,104},{113,120},{... | collective-permute-start | bytes 6291464 | tf_op jit(solution)/shard_map/ppermute | solution.py:264
  16.2 0.3 collective-permute-done.2
  16.5 1.3 broadcast_select_fusion.1
  17.8 2.6 %collective-permute-start.3 = (f32[128,1024]{1,0:T(8,128)S(1)}, f32[128,1024]{1,0:T(8,128)S(1)}, u32[]{:S(2)}, u32[]{:S(2)}) collective-permute-start(f32[128,1024]{1,0:T(8,128)S(1)} %broadcast_select_fusion.1), channel_id=1, source_target_pairs={{0,2},{2,4},{4,6},{6,0},{8,14},{10,8},{12,10},{14,12},{1,3},{3,5},... | collective-permute-start | bytes 1572872 | tf_op jit(solution)/shard_map/ppermute | solution.py:246
  20.4 1.3 broadcast_select_fusion
  21.6 0.6 collective-permute-start.7
  22.2 4.2 %collective-permute-done.3 = f32[128,1024]{1,0:T(8,128)S(1)} collective-permute-done((f32[128,1024]{1,0:T(8,128)S(1)}, f32[128,1024]{1,0:T(8,128)S(1)}, u32[]{:S(2)}, u32[]{:S(2)}) %collective-permute-start.3) | collective-permute-done | bytes 524320 | tf_op jit(solution)/shard_map/ppermute | solution.py:246
  26.5 3.1 %collective-permute-start.4 = (f32[128,1024]{1,0:T(8,128)S(1)}, f32[128,1024]{1,0:T(8,128)}, u32[]{:S(2)}, u32[]{:S(2)}) collective-permute-start(f32[128,1024]{1,0:T(8,128)S(1)} %collective-permute-done.3), channel_id=1, source_target_pairs={{0,2},{2,4},{4,6},{6,0},{8,14},{10,8},{12,10},{14,12},{1,3},{3,5},... | collective-permute-start | bytes 1572872 | tf_op jit(solution)/shard_map/ppermute | solution.py:246
  29.6 2.5 %collective-permute-done.7 = f32[128,1024]{1,0:T(8,128)} collective-permute-done((f32[128,1024]{1,0:T(8,128)S(1)}, f32[128,1024]{1,0:T(8,128)}, u32[]{:S(2)}, u32[]{:S(2)}) %collective-permute-start.7) | collective-permute-done | bytes 524320 | tf_op jit(solution)/shard_map/ppermute | solution.py:246
  32.1 3.2 %collective-permute-start.8 = (f32[128,1024]{1,0:T(8,128)}, f32[128,1024]{1,0:T(8,128)}, u32[]{:S(2)}, u32[]{:S(2)}) collective-permute-start(f32[128,1024]{1,0:T(8,128)} %collective-permute-done.7), channel_id=1, source_target_pairs={{0,2},{2,4},{4,6},{6,0},{8,14},{10,8},{12,10},{14,12},{1,3},{3,5},... | collective-permute-start | bytes 1572872 | tf_op jit(solution)/shard_map/ppermute | solution.py:246
  35.3 2.4 %collective-permute-done.4 = f32[128,1024]{1,0:T(8,128)} collective-permute-done((f32[128,1024]{1,0:T(8,128)S(1)}, f32[128,1024]{1,0:T(8,128)}, u32[]{:S(2)}, u32[]{:S(2)}) %collective-permute-start.4) | collective-permute-done | bytes 524320 | tf_op jit(solution)/shard_map/ppermute | solution.py:246
  37.7 3.2 %collective-permute-start.5 = (f32[128,1024]{1,0:T(8,128)}, f32[128,1024]{1,0:T(8,128)}, u32[]{:S(2)}, u32[]{:S(2)}) collective-permute-start(f32[128,1024]{1,0:T(8,128)} %collective-permute-done.4), channel_id=1, source_target_pairs={{0,2},{2,4},{4,6},{6,0},{8,14},{10,8},{12,10},{14,12},{1,3},{3,5},... | collective-permute-start | bytes 1572872 | tf_op jit(solution)/shard_map/ppermute | solution.py:246
  40.9 0.1 pad_add_fusion.at_ref
  41.0 1.6 %copy-done.1 = f32[1,512,1024]{2,1,0:T(8,128)S(1)} copy-done((f32[1,512,1024]{2,1,0:T(8,128)S(1)}, f32[1,512,1024]{2,1,0:T(8,128)}, u32[]{:S(2)}) %copy-start.1) | copy-done | bytes 2097176
  42.6 2.9 %split_frames.1 = (bf16[512,1024]{1,0:T(8,128)(2,1)S(1)}, bf16[512,1024]{1,0:T(8,128)(2,1)S(1)}, bf16[1024,512]{1,0:T(8,128)(2,1)S(1)}, bf16[1024,512]{1,0:T(8,128)(2,1)S(1)}) custom-call(s32[3]{0:T(128)S(1)} %pad_add_fusion.at_ref, f32[512,1024]{1,0:T(8,128)S(1)} %bitcast.69, f32[512,1024]{1,0:T(8,128)} %collective-permute-done.1.sent), custom_call_target="tpu_custom_call" | custom-call | flops 524288 | bytes 6291456 | tf_op jit(solution)/shard_map/split_frames/pallas_call | solution.py:93
  45.5 1.1 collective-permute-start.9
  46.6 2.5 %collective-permute-done.5 = f32[128,1024]{1,0:T(8,128)} collective-permute-done((f32[128,1024]{1,0:T(8,128)}, f32[128,1024]{1,0:T(8,128)}, u32[]{:S(2)}, u32[]{:S(2)}) %collective-permute-start.5) | collective-permute-done | bytes 524320 | tf_op jit(solution)/shard_map/ppermute | solution.py:246
  49.1 1.4 pad_maximum_fusion.mine
  50.5 8.0 %collective-permute-start.6 = (f32[4,128,1024]{2,1,0:T(8,128)S(1)}, f32[4,128,1024]{2,1,0:T(8,128)S(1)}, u32[]{:S(2)}, u32[]{:S(2)}) collective-permute-start(f32[4,128,1024]{2,1,0:T(8,128)S(1)} %pad_maximum_fusion.mine), channel_id=1, source_target_pairs={{0,8},{8,0},{1,9},{9,1},{2,10},{10,2},{3,11},{11,3},{4,12},{12,4},... | collective-permute-start | bytes 6291464 | tf_op jit(solution)/shard_map/ppermute | solution.py:250
  58.5 1.4 pad_maximum_fusion.1.mine
  59.9 1.4 collective-permute-done.10.sent
  61.3 2.9 %collective-permute-start.11 = (f32[4,128,1024]{2,1,0:T(8,128)S(1)}, f32[4,128,1024]{2,1,0:T(8,128)S(1)}, u32[]{:S(2)}, u32[]{:S(2)}) collective-permute-start(f32[4,128,1024]{2,1,0:T(8,128)S(1)} %pad_maximum_fusion.1.mine), channel_id=1, source_target_pairs={{0,8},{8,0},{1,9},{9,1},{2,10},{10,2},{3,11},{11,3},{4,12},{12,4},... | collective-permute-start | bytes 6291464 | tf_op jit(solution)/shard_map/ppermute | solution.py:250
  64.2 6.1 %first_layer.1 = (bf16[512,1024]{1,0:T(8,128)(2,1)S(1)}, bf16[512,1024]{1,0:T(8,128)(2,1)S(1)}, bf16[1024,512]{1,0:T(8,128)(2,1)S(1)}, bf16[1024,512]{1,0:T(8,128)(2,1)S(1)}, f32[512,1024]{1,0:T(8,128)S(1)}) custom-call(s32[3]{0:T(128)S(1)} %pad_add_fusion.at_ref, bf16[512,1024]{1,0:T(8,128)(2,1)S(1)} %get-tuple-element.38.xh, ...), custom_call_target="tpu_custom_call" | custom-call | flops 3221225472 | bytes 16777216 | tf_op jit(solution)/shard_map/first_layer/pallas_call | solution.py:123
  70.4 5.1 %second_layer.1 = (f32[512,1024]{1,0:T(8,128)S(1)}, bf16[1024,1024]{1,0:T(8,128)(2,1)S(1)}, bf16[1024,1024]{1,0:T(8,128)(2,1)S(1)}) custom-call(s32[3]{0:T(128)S(1)} %pad_add_fusion.at_ref, bf16[512,1024]{1,0:T(8,128)(2,1)S(1)} %get-tuple-element.40.hid_h, bf16[512,1024]{1,0:T(8,128)(2,1)S(1)} %get-tuple-element.41.hid_l, ...), custom_call_target="tpu_custom_call" | custom-call | flops 3221225472 | bytes 12582912 | tf_op jit(solution)/shard_map/second_layer/pallas_call | solution.py:149
  75.4 4.4 %delta_and_second.2 = (f32[4,128,512]{2,1,0:T(8,128)S(1)}, f32[4,128,512]{2,1,0:T(8,128)S(1)}, f32[512,1024]{1,0:T(8,128)S(1)}) custom-call(s32[3]{0:T(128)S(1)} %pad_add_fusion.at_ref, f32[512,1024]{1,0:T(8,128)S(1)} %get-tuple-element.45.out, f32[512,1024]{1,0:T(8,128)S(1)} %bitcast.66, f32[512,1024]{1,0:T(8,128)S(1)} %collective-permute-done.10.sent, ...), custom_call_target="tpu_custom_call" | custom-call | flops 3221225472 | bytes 12582912 | tf_op jit(solution)/shard_map/delta_and_second/pallas_call | solution.py:199
  79.8 0.1 collective-permute-start.18
  79.9 4.6 %delta_and_second.3 = (f32[4,128,512]{2,1,0:T(8,128)S(1)}, f32[4,128,512]{2,1,0:T(8,128)S(1)}, f32[512,1024]{1,0:T(8,128)S(1)}) custom-call(s32[3]{0:T(128)S(1)} %pad_add_fusion.at_ref, f32[512,1024]{1,0:T(8,128)S(1)} %get-tuple-element.45.out, f32[512,1024]{1,0:T(8,128)S(1)} %bitcast.67, f32[512,1024]{1,0:T(8,128)S(1)} %collective-permute-done.10.sent, ...), custom_call_target="tpu_custom_call" | custom-call | flops 3221225472 | bytes 12582912 | tf_op jit(solution)/shard_map/delta_and_second/pallas_call | solution.py:199
  84.6 0.5 collective-permute-start.19
  85.1 4.3 %grad_first.1 = (f32[4,128,1024]{2,1,0:T(8,128)S(1)}, f32[4,128,1024]{2,1,0:T(8,128)S(1)}) custom-call(s32[3]{0:T(128)S(1)} %pad_add_fusion.at_ref, f32[512,1024]{1,0:T(8,128)S(1)} %get-tuple-element.52.back, f32[512,1024]{1,0:T(8,128)S(1)} %get-tuple-element.53.slope, bf16[1024,512]{1,0:T(8,128)(2,1)S(1)} %get-tuple-element.54.xt_h, ...), custom_call_target="tpu_custom_call" | custom-call | flops 3221225472 | bytes 6291456 | tf_op jit(solution)/shard_map/grad_first/pallas_call | solution.py:232
  89.4 0.2 collective-permute-start.12
  89.6 0.4 collective-permute-start.15
  90.0 0.1 collective-permute-start.16
  90.2 0.2 fusion.12
  90.4 0.2 fusion.11
  90.7 1.3 collective-permute-start.20
  92.0 3.2 %collective-permute-done.15 = f32[128,1024]{1,0:T(8,128)S(1)} collective-permute-done((f32[128,1024]{1,0:T(8,128)S(1)}, f32[128,1024]{1,0:T(8,128)S(1)}, u32[]{:S(2)}, u32[]{:S(2)}) %collective-permute-start.15) | collective-permute-done | bytes 524320 | tf_op jit(solution)/shard_map/ppermute | solution.py:250
  95.2 0.2 collective-permute-done.16
  95.5 0.2 collective-permute-start.23
  95.7 3.4 %collective-permute-done.20 = f32[128,1024]{1,0:T(8,128)S(1)} collective-permute-done((f32[128,1024]{1,0:T(8,128)S(1)}, f32[128,1024]{1,0:T(8,128)S(1)}, u32[]{:S(2)}, u32[]{:S(2)}) %collective-permute-start.20) | collective-permute-done | bytes 524320 | tf_op jit(solution)/shard_map/ppermute | solution.py:246
  99.1 2.3 %collective-permute-start.21 = (f32[128,1024]{1,0:T(8,128)S(1)}, f32[128,1024]{1,0:T(8,128)S(1)}, u32[]{:S(2)}, u32[]{:S(2)}) collective-permute-start(f32[128,1024]{1,0:T(8,128)S(1)} %maximum_add_fusion), channel_id=1, source_target_pairs={{0,2},{2,4},{4,6},{6,0},{8,14},{10,8},{12,10},{14,12},{1,3},{3,5},... | collective-permute-start | bytes 1572872 | tf_op jit(solution)/shard_map/ppermute | solution.py:246
  101.5 0.1 collective-permute-start.13
  101.6 0.7 collective-permute-start.17
  102.5 5.1 %collective-permute-done.21 = f32[128,1024]{1,0:T(8,128)S(1)} collective-permute-done((f32[128,1024]{1,0:T(8,128)S(1)}, f32[128,1024]{1,0:T(8,128)S(1)}, u32[]{:S(2)}, u32[]{:S(2)}) %collective-permute-start.21) | collective-permute-done | bytes 524320 | tf_op jit(solution)/shard_map/ppermute | solution.py:246
  107.6 3.4 %collective-permute-start.22 = (f32[128,1024]{1,0:T(8,128)S(1)}, f32[128,1024]{1,0:T(8,128)S(1)}, u32[]{:S(2)}, u32[]{:S(2)}) collective-permute-start(f32[128,1024]{1,0:T(8,128)S(1)} %maximum_add_fusion.1), channel_id=1, source_target_pairs={{0,2},{2,4},{4,6},{6,0},{8,14},{10,8},{12,10},{14,12},{1,3},{3,5},... | collective-permute-start | bytes 1572872 | tf_op jit(solution)/shard_map/ppermute | solution.py:246
  111.0 2.1 %collective-permute-done.13 = f32[128,1024]{1,0:T(8,128)S(1)} collective-permute-done((f32[128,1024]{1,0:T(8,128)S(1)}, f32[128,1024]{1,0:T(8,128)S(1)}, u32[]{:S(2)}, u32[]{:S(2)}) %collective-permute-start.13) | collective-permute-done | bytes 524320 | tf_op jit(solution)/shard_map/ppermute | solution.py:246
  113.2 0.1 fusion.8
  113.3 3.5 %collective-permute-start.14 = (f32[128,1024]{1,0:T(8,128)S(1)}, f32[128,1024]{1,0:T(8,128)S(1)}, u32[]{:S(2)}, u32[]{:S(2)}) collective-permute-start(f32[128,1024]{1,0:T(8,128)S(1)} %fusion.8), channel_id=1, source_target_pairs={{0,2},{2,4},{4,6},{6,0},{8,14},{10,8},{12,10},{14,12},{1,3},{3,5},... | collective-permute-start | bytes 1572872 | tf_op jit(solution)/shard_map/ppermute | solution.py:246
  116.8 0.2 select_multiply_fusion
  117.0 1.8 %collective-permute-done.22 = f32[128,1024]{1,0:T(8,128)S(1)} collective-permute-done((f32[128,1024]{1,0:T(8,128)S(1)}, f32[128,1024]{1,0:T(8,128)S(1)}, u32[]{:S(2)}, u32[]{:S(2)}) %collective-permute-start.22) | collective-permute-done | bytes 524320 | tf_op jit(solution)/shard_map/ppermute | solution.py:246
  118.8 0.1 fusion.4
  118.9 5.5 %collective-permute-done.14 = f32[128,1024]{1,0:T(8,128)S(1)} collective-permute-done((f32[128,1024]{1,0:T(8,128)S(1)}, f32[128,1024]{1,0:T(8,128)S(1)}, u32[]{:S(2)}, u32[]{:S(2)}) %collective-permute-start.14) | collective-permute-done | bytes 524320 | tf_op jit(solution)/shard_map/ppermute | solution.py:246
  124.4 0.1 fusion.6
  124.5 3.2 %collective-permute-start.25 = (f32[128,1024]{1,0:T(8,128)S(1)}, f32[128,1024]{1,0:T(8,128)S(1)}, u32[]{:S(2)}, u32[]{:S(2)}) collective-permute-start(f32[128,1024]{1,0:T(8,128)S(1)} %fusion.6), channel_id=1, source_target_pairs={{0,2},{2,4},{4,6},{6,0},{8,14},{10,8},{12,10},{14,12},{1,3},{3,5},... | collective-permute-start | bytes 1572872 | tf_op jit(solution)/shard_map/ppermute | solution.py:246
  127.7 1.9 %collective-permute-start.27 = (f32[128,1024]{1,0:T(8,128)S(1)}, f32[128,1024]{1,0:T(8,128)S(1)}, u32[]{:S(2)}, u32[]{:S(2)}) collective-permute-start(f32[128,1024]{1,0:T(8,128)S(1)} %fusion.4), channel_id=1, source_target_pairs={{1,8},{17,24},{33,40},{49,56},{65,72},{81,88},{97,104},{113,120},{... | collective-permute-start | bytes 1572872 | tf_op jit(solution)/shard_map/ppermute | solution.py:264
  129.6 4.2 %collective-permute-done.25 = f32[128,1024]{1,0:T(8,128)S(1)} collective-permute-done((f32[128,1024]{1,0:T(8,128)S(1)}, f32[128,1024]{1,0:T(8,128)S(1)}, u32[]{:S(2)}, u32[]{:S(2)}) %collective-permute-start.25) | collective-permute-done | bytes 524320 | tf_op jit(solution)/shard_map/ppermute | solution.py:246
  133.8 0.2 fusion.3
  134.0 6.2 %collective-permute-start.26 = (f32[128,1024]{1,0:T(8,128)S(1)}, f32[128,1024]{1,0:T(8,128)S(1)}, u32[]{:S(2)}, u32[]{:S(2)}) collective-permute-start(f32[128,1024]{1,0:T(8,128)S(1)} %fusion.3), channel_id=1, source_target_pairs={{1,8},{17,24},{33,40},{49,56},{65,72},{81,88},{97,104},{113,120},{... | collective-permute-start | bytes 1572872 | tf_op jit(solution)/shard_map/ppermute | solution.py:264
  140.2 0.9 add_bitcast_fusion
  141.1 5.9 %collective-permute-done.26 = f32[128,1024]{1,0:T(8,128)S(1)} collective-permute-done((f32[128,1024]{1,0:T(8,128)S(1)}, f32[128,1024]{1,0:T(8,128)S(1)}, u32[]{:S(2)}, u32[]{:S(2)}) %collective-permute-start.26) | collective-permute-done | bytes 524320 | tf_op jit(solution)/shard_map/ppermute | solution.py:264
  147.0 0.9 add_bitcast_fusion.1
  (36 shorter events, 0.5 us)
Async XLA Ops:
  0.6 10.0 %collective-permute-start = (f32[128,1024]{1,0:T(8,128)}, f32[128,1024]{1,0:T(8,128)}, u32[]{:S(2)}, u32[]{:S(2)}) collective-permute-start(f32[128,1024]{1,0:T(8,128)} %bitcast.70), channel_id=1, source_target_pairs={{1,8},{17,24},{33,40},{49,56},{65,72},{81,88},{97,104},{113,120},{... | collective-permute-start | bytes 1572872 | tf_op jit(solution)/shard_map/ppermute | solution.py:264
  3.4 13.1 %collective-permute-start.2 = (f32[128,1024]{1,0:T(8,128)}, f32[128,1024]{1,0:T(8,128)S(1)}, u32[]{:S(2)}, u32[]{:S(2)}) collective-permute-start(f32[128,1024]{1,0:T(8,128)} %bitcast.72), channel_id=1, source_target_pairs={{1,8},{17,24},{33,40},{49,56},{65,72},{81,88},{97,104},{113,120},{... | collective-permute-start | bytes 1572872 | tf_op jit(solution)/shard_map/ppermute | solution.py:264
  10.6 30.4 %collective-permute-start.1 = (f32[512,1024]{1,0:T(8,128)}, f32[512,1024]{1,0:T(8,128)}, u32[]{:S(2)}, u32[]{:S(2)}) collective-permute-start(f32[512,1024]{1,0:T(8,128)} %bitcast.68), channel_id=1, source_target_pairs={{1,8},{17,24},{33,40},{49,56},{65,72},{81,88},{97,104},{113,120},{... | collective-permute-start | bytes 6291464 | tf_op jit(solution)/shard_map/ppermute | solution.py:264
  14.2 47.1 %collective-permute-start.10 = (f32[512,1024]{1,0:T(8,128)}, f32[512,1024]{1,0:T(8,128)S(1)}, u32[]{:S(2)}, u32[]{:S(2)}) collective-permute-start(f32[512,1024]{1,0:T(8,128)} %bitcast.65), channel_id=1, source_target_pairs={{1,8},{17,24},{33,40},{49,56},{65,72},{81,88},{97,104},{113,120},{... | collective-permute-start | bytes 6291464 | tf_op jit(solution)/shard_map/ppermute | solution.py:264
  16.5 1.3 copy-start.4
  17.8 8.7 %collective-permute-start.3 = (f32[128,1024]{1,0:T(8,128)S(1)}, f32[128,1024]{1,0:T(8,128)S(1)}, u32[]{:S(2)}, u32[]{:S(2)}) collective-permute-start(f32[128,1024]{1,0:T(8,128)S(1)} %broadcast_select_fusion.1), channel_id=1, source_target_pairs={{0,2},{2,4},{4,6},{6,0},{8,14},{10,8},{12,10},{14,12},{1,3},{3,5},... | collective-permute-start | bytes 1572872 | tf_op jit(solution)/shard_map/ppermute | solution.py:246
  21.6 10.5 %collective-permute-start.7 = (f32[128,1024]{1,0:T(8,128)S(1)}, f32[128,1024]{1,0:T(8,128)}, u32[]{:S(2)}, u32[]{:S(2)}) collective-permute-start(f32[128,1024]{1,0:T(8,128)S(1)} %broadcast_select_fusion), channel_id=1, source_target_pairs={{0,2},{2,4},{4,6},{6,0},{8,14},{10,8},{12,10},{14,12},{1,3},{3,5},... | collective-permute-start | bytes 1572872 | tf_op jit(solution)/shard_map/ppermute | solution.py:246
  26.5 5.6 %copy-start.6 = (f32[128,1024]{1,0:T(8,128)}, f32[128,1024]{1,0:T(8,128)S(1)}, u32[]{:S(2)}) copy-start(f32[128,1024]{1,0:T(8,128)S(1)} %collective-permute-done.3) | copy-start | bytes 1572868
  26.5 11.2 %collective-permute-start.4 = (f32[128,1024]{1,0:T(8,128)S(1)}, f32[128,1024]{1,0:T(8,128)}, u32[]{:S(2)}, u32[]{:S(2)}) collective-permute-start(f32[128,1024]{1,0:T(8,128)S(1)} %collective-permute-done.3), channel_id=1, source_target_pairs={{0,2},{2,4},{4,6},{6,0},{8,14},{10,8},{12,10},{14,12},{1,3},{3,5},... | collective-permute-start | bytes 1572872 | tf_op jit(solution)/shard_map/ppermute | solution.py:246
  32.1 13.4 %collective-permute-start.8 = (f32[128,1024]{1,0:T(8,128)}, f32[128,1024]{1,0:T(8,128)}, u32[]{:S(2)}, u32[]{:S(2)}) collective-permute-start(f32[128,1024]{1,0:T(8,128)} %collective-permute-done.7), channel_id=1, source_target_pairs={{0,2},{2,4},{4,6},{6,0},{8,14},{10,8},{12,10},{14,12},{1,3},{3,5},... | collective-permute-start | bytes 1572872 | tf_op jit(solution)/shard_map/ppermute | solution.py:246
  37.7 11.3 %collective-permute-start.5 = (f32[128,1024]{1,0:T(8,128)}, f32[128,1024]{1,0:T(8,128)}, u32[]{:S(2)}, u32[]{:S(2)}) collective-permute-start(f32[128,1024]{1,0:T(8,128)} %collective-permute-done.4), channel_id=1, source_target_pairs={{0,2},{2,4},{4,6},{6,0},{8,14},{10,8},{12,10},{14,12},{1,3},{3,5},... | collective-permute-start | bytes 1572872 | tf_op jit(solution)/shard_map/ppermute | solution.py:246
  41.0 1.6 %copy-start.1 = (f32[1,512,1024]{2,1,0:T(8,128)S(1)}, f32[1,512,1024]{2,1,0:T(8,128)}, u32[]{:S(2)}) copy-start(f32[1,512,1024]{2,1,0:T(8,128)} %param.4) | copy-start | bytes 6291460
  42.6 6.4 %copy-start.7 = (f32[128,1024]{1,0:T(8,128)S(1)}, f32[128,1024]{1,0:T(8,128)}, u32[]{:S(2)}) copy-start(f32[128,1024]{1,0:T(8,128)} %copy-done.6) | copy-start | bytes 1572868
  45.5 13.0 %collective-permute-start.9 = (f32[128,1024]{1,0:T(8,128)}, f32[128,1024]{1,0:T(8,128)S(1)}, u32[]{:S(2)}, u32[]{:S(2)}) collective-permute-start(f32[128,1024]{1,0:T(8,128)} %collective-permute-done.8), channel_id=1, source_target_pairs={{0,2},{2,4},{4,6},{6,0},{8,14},{10,8},{12,10},{14,12},{1,3},{3,5},... | collective-permute-start | bytes 1572872 | tf_op jit(solution)/shard_map/ppermute | solution.py:246
  50.5 13.7 %collective-permute-start.6 = (f32[4,128,1024]{2,1,0:T(8,128)S(1)}, f32[4,128,1024]{2,1,0:T(8,128)S(1)}, u32[]{:S(2)}, u32[]{:S(2)}) collective-permute-start(f32[4,128,1024]{2,1,0:T(8,128)S(1)} %pad_maximum_fusion.mine), channel_id=1, source_target_pairs={{0,8},{8,0},{1,9},{9,1},{2,10},{10,2},{3,11},{11,3},{4,12},{12,4},... | collective-permute-start | bytes 6291464 | tf_op jit(solution)/shard_map/ppermute | solution.py:250
  61.3 9.0 %collective-permute-start.11 = (f32[4,128,1024]{2,1,0:T(8,128)S(1)}, f32[4,128,1024]{2,1,0:T(8,128)S(1)}, u32[]{:S(2)}, u32[]{:S(2)}) collective-permute-start(f32[4,128,1024]{2,1,0:T(8,128)S(1)} %pad_maximum_fusion.1.mine), channel_id=1, source_target_pairs={{0,8},{8,0},{1,9},{9,1},{2,10},{10,2},{3,11},{11,3},{4,12},{12,4},... | collective-permute-start | bytes 6291464 | tf_op jit(solution)/shard_map/ppermute | solution.py:250
  70.4 5.1 %copy-start = (f32[1,512,1024]{2,1,0:T(8,128)S(1)}, f32[1,512,1024]{2,1,0:T(8,128)}, u32[]{:S(2)}) copy-start(f32[1,512,1024]{2,1,0:T(8,128)} %param.5) | copy-start | bytes 6291460
  79.8 10.3 %collective-permute-start.18 = (f32[4,128,512]{2,1,0:T(8,128)S(1)}, f32[4,128,512]{2,1,0:T(8,128)S(1)}, u32[]{:S(2)}, u32[]{:S(2)}) collective-permute-start(f32[4,128,512]{2,1,0:T(8,128)S(1)} %get-tuple-element.62), channel_id=1, source_target_pairs={{0,8},{8,0},{1,9},{9,1},{2,10},{10,2},{3,11},{11,3},{4,12},{12,4},... | collective-permute-start | bytes 3145736 | tf_op jit(solution)/shard_map/ppermute | solution.py:250
  84.6 5.8 %collective-permute-start.19 = (f32[4,128,512]{2,1,0:T(8,128)S(1)}, f32[4,128,512]{2,1,0:T(8,128)S(1)}, u32[]{:S(2)}, u32[]{:S(2)}) collective-permute-start(f32[4,128,512]{2,1,0:T(8,128)S(1)} %get-tuple-element.64), channel_id=1, source_target_pairs={{0,8},{8,0},{1,9},{9,1},{2,10},{10,2},{3,11},{11,3},{4,12},{12,4},... | collective-permute-start | bytes 3145736 | tf_op jit(solution)/shard_map/ppermute | solution.py:250
  85.1 4.5 %copy-start.5 = (f32[128,1024]{1,0:T(8,128)S(1)}, f32[128,1024]{1,0:T(8,128)}, u32[]{:S(2)}) copy-start(f32[128,1024]{1,0:T(8,128)} %copy-done.4) | copy-start | bytes 1572868
  89.4 12.0 %collective-permute-start.12 = (f32[4,128,1024]{2,1,0:T(8,128)S(1)}, f32[4,128,1024]{2,1,0:T(8,128)S(1)}, u32[]{:S(2)}, u32[]{:S(2)}) collective-permute-start(f32[4,128,1024]{2,1,0:T(8,128)S(1)} %get-tuple-element.57), channel_id=1, source_target_pairs={{0,8},{8,0},{1,9},{9,1},{2,10},{10,2},{3,11},{11,3},{4,12},{12,4},... | collective-permute-start | bytes 6291464 | tf_op jit(solution)/shard_map/ppermute | solution.py:250
  89.6 5.6 %collective-permute-start.15 = (f32[128,1024]{1,0:T(8,128)S(1)}, f32[128,1024]{1,0:T(8,128)S(1)}, u32[]{:S(2)}, u32[]{:S(2)}) collective-permute-start(f32[128,1024]{1,0:T(8,128)S(1)} %copy-done.5), channel_id=1, source_target_pairs={{0,8},{8,0},{1,9},{9,1},{2,10},{10,2},{3,11},{11,3},{4,12},{12,4},... | collective-permute-start | bytes 1572872 | tf_op jit(solution)/shard_map/ppermute | solution.py:250
  90.0 5.4 %collective-permute-start.16 = (f32[128,1024]{1,0:T(8,128)}, f32[128,1024]{1,0:T(8,128)S(1)}, u32[]{:S(2)}, u32[]{:S(2)}) collective-permute-start(f32[128,1024]{1,0:T(8,128)} %collective-permute-done), channel_id=1, source_target_pairs={{0,8},{8,0},{1,9},{9,1},{2,10},{10,2},{3,11},{11,3},{4,12},{12,4},... | collective-permute-start | bytes 1572872 | tf_op jit(solution)/shard_map/ppermute | solution.py:250
  90.4 1.6 %copy-start.2 = (f32[1,128,1024]{2,1,0:T(8,128)S(1)}, f32[1,128,1024]{2,1,0:T(8,128)}, u32[]{:S(2)}) copy-start(f32[1,128,1024]{2,1,0:T(8,128)} %param.7) | copy-start | bytes 1572868
  90.6 4.9 %copy-start.3 = (f32[1,128,1024]{2,1,0:T(8,128)S(1)}, f32[1,128,1024]{2,1,0:T(8,128)}, u32[]{:S(2)}) copy-start(f32[1,128,1024]{2,1,0:T(8,128)} %param.6) | copy-start | bytes 1572868
  90.7 8.4 %collective-permute-start.20 = (f32[128,1024]{1,0:T(8,128)S(1)}, f32[128,1024]{1,0:T(8,128)S(1)}, u32[]{:S(2)}, u32[]{:S(2)}) collective-permute-start(f32[128,1024]{1,0:T(8,128)S(1)} %pad_maximum_fusion.3), channel_id=1, source_target_pairs={{0,2},{2,4},{4,6},{6,0},{8,14},{10,8},{12,10},{14,12},{1,3},{3,5},... | collective-permute-start | bytes 1572872 | tf_op jit(solution)/shard_map/ppermute | solution.py:246
  92.0 10.3 %collective-permute-start.24 = (f32[128,1024]{1,0:T(8,128)S(1)}, f32[128,1024]{1,0:T(8,128)S(1)}, u32[]{:S(2)}, u32[]{:S(2)}) collective-permute-start(f32[128,1024]{1,0:T(8,128)S(1)} %bitcast.71), channel_id=1, source_target_pairs={{0,8},{8,0},{1,9},{9,1},{2,10},{10,2},{3,11},{11,3},{4,12},{12,4},... | collective-permute-start | bytes 1572872 | tf_op jit(solution)/shard_map/ppermute | solution.py:250
  95.5 6.9 %collective-permute-start.23 = (f32[128,1024]{1,0:T(8,128)S(1)}, f32[128,1024]{1,0:T(8,128)S(1)}, u32[]{:S(2)}, u32[]{:S(2)}) collective-permute-start(f32[128,1024]{1,0:T(8,128)S(1)} %bitcast.73), channel_id=1, source_target_pairs={{0,8},{8,0},{1,9},{9,1},{2,10},{10,2},{3,11},{11,3},{4,12},{12,4},... | collective-permute-start | bytes 1572872 | tf_op jit(solution)/shard_map/ppermute | solution.py:250
  99.1 8.4 %collective-permute-start.21 = (f32[128,1024]{1,0:T(8,128)S(1)}, f32[128,1024]{1,0:T(8,128)S(1)}, u32[]{:S(2)}, u32[]{:S(2)}) collective-permute-start(f32[128,1024]{1,0:T(8,128)S(1)} %maximum_add_fusion), channel_id=1, source_target_pairs={{0,2},{2,4},{4,6},{6,0},{8,14},{10,8},{12,10},{14,12},{1,3},{3,5},... | collective-permute-start | bytes 1572872 | tf_op jit(solution)/shard_map/ppermute | solution.py:246
  101.5 11.7 %collective-permute-start.13 = (f32[128,1024]{1,0:T(8,128)S(1)}, f32[128,1024]{1,0:T(8,128)S(1)}, u32[]{:S(2)}, u32[]{:S(2)}) collective-permute-start(f32[128,1024]{1,0:T(8,128)S(1)} %fusion.9), channel_id=1, source_target_pairs={{0,2},{2,4},{4,6},{6,0},{8,14},{10,8},{12,10},{14,12},{1,3},{3,5},... | collective-permute-start | bytes 1572872 | tf_op jit(solution)/shard_map/ppermute | solution.py:246
  101.6 15.2 %collective-permute-start.17 = (f32[2,128,1024]{2,1,0:T(8,128)S(1)}, f32[2,128,1024]{2,1,0:T(8,128)S(1)}, u32[]{:S(2)}, u32[]{:S(2)}) collective-permute-start(f32[2,128,1024]{2,1,0:T(8,128)S(1)} %pad_maximum_fusion.2), channel_id=1, source_target_pairs={{9,16},{25,32},{41,48},{57,64},{73,80},{89,96},{105,112},{121,128}... | collective-permute-start | bytes 3145736 | tf_op jit(solution)/shard_map/ppermute | solution.py:264
  107.6 11.2 %collective-permute-start.22 = (f32[128,1024]{1,0:T(8,128)S(1)}, f32[128,1024]{1,0:T(8,128)S(1)}, u32[]{:S(2)}, u32[]{:S(2)}) collective-permute-start(f32[128,1024]{1,0:T(8,128)S(1)} %maximum_add_fusion.1), channel_id=1, source_target_pairs={{0,2},{2,4},{4,6},{6,0},{8,14},{10,8},{12,10},{14,12},{1,3},{3,5},... | collective-permute-start | bytes 1572872 | tf_op jit(solution)/shard_map/ppermute | solution.py:246
  113.3 11.1 %collective-permute-start.14 = (f32[128,1024]{1,0:T(8,128)S(1)}, f32[128,1024]{1,0:T(8,128)S(1)}, u32[]{:S(2)}, u32[]{:S(2)}) collective-permute-start(f32[128,1024]{1,0:T(8,128)S(1)} %fusion.8), channel_id=1, source_target_pairs={{0,2},{2,4},{4,6},{6,0},{8,14},{10,8},{12,10},{14,12},{1,3},{3,5},... | collective-permute-start | bytes 1572872 | tf_op jit(solution)/shard_map/ppermute | solution.py:246
  124.5 9.3 %collective-permute-start.25 = (f32[128,1024]{1,0:T(8,128)S(1)}, f32[128,1024]{1,0:T(8,128)S(1)}, u32[]{:S(2)}, u32[]{:S(2)}) collective-permute-start(f32[128,1024]{1,0:T(8,128)S(1)} %fusion.6), channel_id=1, source_target_pairs={{0,2},{2,4},{4,6},{6,0},{8,14},{10,8},{12,10},{14,12},{1,3},{3,5},... | collective-permute-start | bytes 1572872 | tf_op jit(solution)/shard_map/ppermute | solution.py:246
  127.7 12.5 %collective-permute-start.27 = (f32[128,1024]{1,0:T(8,128)S(1)}, f32[128,1024]{1,0:T(8,128)S(1)}, u32[]{:S(2)}, u32[]{:S(2)}) collective-permute-start(f32[128,1024]{1,0:T(8,128)S(1)} %fusion.4), channel_id=1, source_target_pairs={{1,8},{17,24},{33,40},{49,56},{65,72},{81,88},{97,104},{113,120},{... | collective-permute-start | bytes 1572872 | tf_op jit(solution)/shard_map/ppermute | solution.py:264
  134.0 13.0 %collective-permute-start.26 = (f32[128,1024]{1,0:T(8,128)S(1)}, f32[128,1024]{1,0:T(8,128)S(1)}, u32[]{:S(2)}, u32[]{:S(2)}) collective-permute-start(f32[128,1024]{1,0:T(8,128)S(1)} %fusion.3), channel_id=1, source_target_pairs={{1,8},{17,24},{33,40},{49,56},{65,72},{81,88},{97,104},{113,120},{... | collective-permute-start | bytes 1572872 | tf_op jit(solution)/shard_map/ppermute | solution.py:264
